TPU v7x, 32 devices: a whole 2x2x4 slice. The times are simulated.
32 devices in a mesh: groups: 2 (over y), param: 8 (over z, x), ex: 2 (over core).
Axes of the slice: x: 2, y: 2, z: 4, core: 2. Of those that a mesh axis runs over, the one named last changes fastest.
Arguments:
- g_train: bfloat16 [2048, 65536], P(('groups', 'ex'), 'param'), parts along dimension 0, may hold values from -6 to 6
- g_target: bfloat16 [1024, 65536], P(('groups', 'ex'), 'param'), parts along dimension 0, may hold values from -6 to 6
- projection: bfloat16 [65536, 4096], P('param'), may hold values from -0.03125 to 0.03125
- kernel_inv: bfloat16 [8192, 4096], P('groups', 'param'), parts along dimension 0, may hold values from -0.09375 to 0.09375
Outputs:
- scores: float32 [2048, 512], P(('groups', 'ex'), 'param'), parts along dimension 0
There are 2 independent parts, one for each index of `groups`. A program takes and returns all parts, laid end to end along the dimension named above; an argument that names none is the same for every part. Nothing has to cross between parts.
All inputs are finite; a program needn't handle non-finite values.
Results may differ from a plain program's by a relative error of at most 0.0041.
Values may be sent and summed in bfloat16 or wider, within the bound.
No kernel may reach another device: no remote copies, remote signals or barrier semaphores. Data moves between devices by JAX's collectives and lax.ppermute only.
A program may use at most 192 MiB of HBM per device.

v0:
```python
import math

import jax
import jax.numpy as jnp
from jax import lax
from jax.sharding import PartitionSpec as P

K = 4096


def on_device(g_train, g_target, projection, kernel_inv):
    factor = 1.0 / math.sqrt(K)
    target_part = jnp.dot(g_target, projection, preferred_element_type=jnp.float32)
    target_feat = lax.psum_scatter(target_part, "param", scatter_dimension=1, tiled=True).astype(
        jnp.bfloat16
    )
    target_full = lax.all_gather(target_feat, "param", axis=1, tiled=True)
    every_target = lax.all_gather(target_full, "ex", axis=0, tiled=True)
    folded = jnp.dot(every_target, kernel_inv, preferred_element_type=jnp.float32).astype(
        jnp.bfloat16
    )
    train_part = jnp.dot(g_train, projection, preferred_element_type=jnp.float32)
    train_feat = lax.psum_scatter(train_part, "param", scatter_dimension=1, tiled=True)
    partial_value = jnp.dot(
        train_feat, folded.astype(jnp.float32).T, precision=lax.Precision.HIGHEST
    )
    return lax.psum_scatter(partial_value * factor, "param", scatter_dimension=1, tiled=True)


def solution(mesh):
    placed = (
        P(("groups", "ex"), "param"),
        P(("groups", "ex"), "param"),
        P("param", None),
        P("groups", "param"),
    )
    return jax.shard_map(
        on_device,
        mesh=mesh,
        in_specs=placed,
        out_specs=P(("groups", "ex"), "param"),
        check_vma=False,
    )
```

profile of v0, /device:TPU:0, one launch (start us, length us, event | category | flops | bytes accessed | tf_op | source)
XLA Modules:
  0.0 446.2 jit_solution(11242666827502364846)
XLA Ops:
  6.5 0.0 reduce-scatter.6.cloned.1.call-start
  6.5 28.5 %fusion.1 = f32[256,4096]{1,0:T(8,128)} fusion(bf16[256,8192]{1,0:T(8,128)(2,1)} %param.5, bf16[8192,4096]{1,0:T(8,128)(2,1)} %param.6), kind=kOutput, calls=%fused_computation.3 | convolution fusion | flops 17179869184 | bytes 75497472 | tf_op jit(solution)/shard_map/dot_general | solution.py:13
  35.1 0.0 reduce-scatter.6.cloned.1.call-update
  35.1 0.0 all-gather.3.cloned.1.call-start
  35.1 91.3 %reduce-scatter.6.cloned.1.call-done = f32[256,512]{1,0:T(8,128)} async-done(((f32[256,4096]{1,0:T(8,128)}), f32[256,512]{1,0:T(8,128)}) %reduce-scatter.6.cloned.1.call-update) | async-done | bytes 524304 | tf_op jit(solution)/shard_map/reduce_scatter | solution.py:14
  126.4 1.8 convert_element_type.7
  128.2 0.0 all-gather.3.cloned.1.call-update
  128.2 0.0 all-gather.5.cloned.1.call-start
  128.3 51.3 %all-gather.3.cloned.1.call-done = bf16[256,4096]{1,0:T(8,128)(2,1)} async-done(((bf16[256,512]{1,0:T(8,128)(2,1)}), bf16[256,4096]{1,0:T(8,128)(2,1)}) %all-gather.3.cloned.1.call-update) | async-done | bytes 2097168 | tf_op jit(solution)/shard_map/all_gather | solution.py:17
  179.5 0.0 all-gather.5.cloned.1.call-update
  179.5 0.0 reduce-scatter.4.cloned.1.call-start
  179.6 46.0 %fusion = f32[512,4096]{1,0:T(8,128)} fusion(bf16[512,8192]{1,0:T(8,128)(2,1)} %param.4, bf16[8192,4096]{1,0:T(8,128)(2,1)} %param.6), kind=kOutput, calls=%fused_computation.2 | convolution fusion | flops 34359738368 | bytes 83886080 | tf_op jit(solution)/shard_map/dot_general | solution.py:22
  225.6 0.0 reduce-scatter.4.cloned.1.call-update
  225.6 0.0 reduce-scatter.8.cloned.1.call-start
  225.7 0.0 all-gather.5.cloned.1.call-done
  225.7 5.8 %convolution_convert_fusion = bf16[512,512]{1,0:T(8,128)(2,1)S(1)} fusion(bf16[512,4096]{1,0:T(8,128)(2,1)} %all-gather.5.cloned.1.call-done, bf16[4096,512]{1,0:T(8,128)(2,1)} %param.7), kind=kOutput, calls=%fused_computation.1 | convolution fusion | flops 2147745792 | bytes 8912896 | tf_op jit(solution)/shard_map/dot_general | solution.py:19
  231.5 141.6 %reduce-scatter.4.cloned.1.call-done = f32[512,512]{1,0:T(8,128)} async-done(((f32[512,4096]{1,0:T(8,128)}), f32[512,512]{1,0:T(8,128)}) %reduce-scatter.4.cloned.1.call-update) | async-done | bytes 1048592 | tf_op jit(solution)/shard_map/reduce_scatter | solution.py:23
  373.1 3.3 convolution_multiply_fusion
  376.3 0.0 reduce-scatter.8.cloned.1.call-update
  376.4 63.3 %reduce-scatter.8.cloned.1.call-done = f32[512,64]{0,1:T(8,128)} async-done(((f32[512,512]{0,1:T(8,128)}), f32[512,64]{0,1:T(8,128)}) %reduce-scatter.8.cloned.1.call-update) | async-done | bytes 131088 | tf_op jit(solution)/shard_map/reduce_scatter | solution.py:27
Async XLA Ops:
  6.5 119.9 %reduce-scatter.6.cloned.1.call-start = ((), (), s32[]{:S(2)}) async-start(), calls=%async_computation.4 | async-start | bytes 4718592 | tf_op jit(solution)/shard_map/reduce_scatter | solution.py:14
  35.1 144.4 %all-gather.3.cloned.1.call-start = ((), (), s32[]{:S(2)}) async-start(), calls=%async_computation.5 | async-start | bytes 2359296 | tf_op jit(solution)/shard_map/all_gather | solution.py:17
  128.2 97.5 %all-gather.5.cloned.1.call-start = ((), (), s32[]{:S(2)}) async-start(), calls=%async_computation.6 | async-start | bytes 6291456 | tf_op jit(solution)/shard_map/all_gather | solution.py:18
  179.5 193.6 %reduce-scatter.4.cloned.1.call-start = ((), (), s32[]{:S(2)}) async-start(), calls=%async_computation.3 | async-start | bytes 9437184 | tf_op jit(solution)/shard_map/reduce_scatter | solution.py:23
  225.6 214.1 %reduce-scatter.8.cloned.1.call-start = ((), (), s32[]{:S(2)}) async-start(), calls=%async_computation.7 | async-start | bytes 1179648 | tf_op jit(solution)/shard_map/reduce_scatter | solution.py:27
Sparse Core Ops, SparseCore 0:
  35.2 91.1 reduce-scatter.5
  128.6 50.8 all-gather.2
  181.1 11.8 all-gather.4
  225.7 147.3 reduce-scatter.3
  376.5 63.1 reduce-scatter.7
where the time goes:
time: 446 us
  waiting for transfers between devices  348 us (78%)
  matrix products  83.6 us (19%)
  between operations  13.2 us (3%)
    reduce_scatter x1, waiting for transfers between devices, on_device(): lax.psum_scatter(train_part, 'param', scatter_dimension=1, tiled=True)  142 us
    reduce_scatter x1, waiting for transfers between devices, on_device(): lax.psum_scatter(target_part, 'param', scatter_dimension=1, tiled=True)  91.3 us
    reduce_scatter x1, waiting for transfers between devices, on_device(): lax.psum_scatter(partial_value * factor, 'param', scatter_dimension=1, ti...  63.3 us
    all_gather x1, waiting for transfers between devices, on_device(): target_full = lax.all_gather(target_feat, 'param', axis=1, tiled=True)  51.3 us
    dot_general x1, matrix products, on_device(): jnp.dot(g_train, projection, preferred_element_type=jnp.float32)  46 us
    dot_general x1, matrix products, on_device(): jnp.dot(g_target, projection, preferred_element_type=jnp.float32)  28.5 us
  transfers between devices with their start and end apart: 5, of which 4 were waited for; matrix products, arithmetic and copies ran while one was open for 12% of the time, Pallas kernels for 0%

commit v1 on v0

v1 whole, which is shorter than its diff:
```python
import math

import jax
import jax.numpy as jnp
from jax import lax
from jax.experimental import pallas as pl
from jax.experimental.pallas import tpu as pltpu
from jax.sharding import PartitionSpec as P

BOTH = ("param", "ex")
SCALE_ROWS = 16


def hop_order(bits):
    low = max(1, bits // 3)
    plain = list(range(bits))
    return [plain, plain[low : 2 * low] + plain[:low] + plain[2 * low :]]


class Cube:
    def __init__(self, n, cores):
        self.n = n
        self.bits = n.bit_length() - 1
        two = hop_order(self.bits)
        self.orders = [two[e % 2] for e in range(cores)]
        self.me = lax.axis_index("param")
        self.core = lax.axis_index("ex")
        self.perms = [
            [
                (p * cores + e, (p ^ (1 << self.orders[e][h])) * cores + e)
                for p in range(n)
                for e in range(cores)
            ]
            for h in range(self.bits)
        ]
        masks = [
            [
                sum(((i >> (self.bits - 1 - h)) & 1) << self.orders[e][h] for h in range(self.bits))
                for i in range(n)
            ]
            for e in range(cores)
        ]
        self.blocks = jnp.bitwise_xor(self.me, jnp.array(masks, jnp.int32)[self.core])
        table = jnp.array(self.orders, jnp.int32)[self.core]
        self.bit = [jnp.bitwise_and(jnp.right_shift(self.me, table[h]), 1) for h in range(self.bits)]

    def swap(self, value, hop):
        return lax.ppermute(value, BOTH, self.perms[hop])


def pow2(k):
    return jnp.exp2(k)


def exponent(top):
    k = jnp.ceil(jnp.log2(jnp.maximum(top, 1e-37)))
    return jnp.clip(k, -110.0, 100.0)


def pack(value, k):
    body = (value * pow2(14.0 - k)).astype(jnp.float16)
    tail = jnp.full((SCALE_ROWS, value.shape[1]), k, jnp.float16)
    return jnp.concatenate([body, tail], axis=0)


def unpack(message):
    rows = message.shape[0] - SCALE_ROWS
    k = message[rows, 0].astype(jnp.float32)
    return message[:rows].astype(jnp.float32) * pow2(k - 14.0), k


def reduce_columns(cube, value):
    k = exponent(jnp.max(jnp.abs(value)))
    for hop in range(cube.bits):
        half = value.shape[1] // 2
        first, second = value[:, :half], value[:, half:]
        low = cube.bit[hop] == 0
        got, other = unpack(cube.swap(pack(jnp.where(low, second, first), k), hop))
        value = jnp.where(low, first, second) + got
        k = jnp.maximum(k, other) + 1.0
    return value


def gather_columns(cube, value):
    for hop in reversed(range(cube.bits)):
        got = cube.swap(value, hop)
        low = cube.bit[hop] == 0
        value = jnp.where(
            low, jnp.concatenate([value, got], axis=1), jnp.concatenate([got, value], axis=1)
        )
    return value


def score_kernel(parts, scale, blocks_ref, *refs):
    projection, (folded, own, other, out_own, out_other) = refs[:parts], refs[parts:]
    width = projection[0].shape[1]
    products = None
    for i in range(parts):
        part = lax.dot_general(
            projection[i][...],
            folded[:, i * width : (i + 1) * width],
            (((1,), (1,)), ((), ())),
            preferred_element_type=jnp.float32,
        )
        products = part if products is None else products + part
    weights = (products * scale).astype(jnp.bfloat16)

    @pl.when(pl.program_id(0) == 0)
    def _():
        out_own[...] = jnp.zeros_like(out_own)
        out_other[...] = jnp.zeros_like(out_other)

    for grad, out in ((own, out_own), (other, out_other)):
        out[...] += lax.dot_general(
            weights, grad[...], (((0,), (1,)), ((), ())), preferred_element_type=jnp.float32
        )


def score_terms(projection, folded, own, other, blocks, parts, scale):
    rows, targets, train = projection.shape[0], folded.shape[0], own.shape[0]
    step = min(512, rows)
    width = folded.shape[1] // parts

    def column(i):
        return pl.BlockSpec((step, width), lambda r, b: (r, b[i]))

    grad = pl.BlockSpec((train, step), lambda r, b: (0, r))
    out = pl.BlockSpec((targets, train), lambda r, b: (0, 0))
    shape = jax.ShapeDtypeStruct((targets, train), jnp.float32)
    flops = 2 * rows * targets * (folded.shape[1] + 2 * train)
    return pl.pallas_call(
        lambda *refs: score_kernel(parts, scale, *refs),
        grid_spec=pltpu.PrefetchScalarGridSpec(
            num_scalar_prefetch=1,
            grid=(rows // step,),
            in_specs=[column(i) for i in range(parts)]
            + [pl.BlockSpec(folded.shape, lambda r, b: (0, 0)), grad, grad],
            out_specs=[out, out],
        ),
        out_shape=[shape, shape],
        compiler_params=pltpu.CompilerParams(vmem_limit_bytes=48 * 2**20),
        cost_estimate=pl.CostEstimate(
            flops=flops,
            bytes_accessed=2 * rows * (folded.shape[1] + 2 * train),
            transcendentals=0,
        ),
    )(blocks, *([projection] * parts), folded, own, other)


def on_device(n, cores, g_train, g_target, projection, kernel_inv):
    cube = Cube(n, cores)
    features = projection.shape[1]
    scale = 1.0 / math.sqrt(features)
    swap_cores = [(e, e ^ 1) for e in range(cores)]
    g_other = lax.ppermute(g_train, "ex", swap_cores)

    chunks = 2
    width = features // chunks
    summed = None
    for c in range(chunks):
        part = jnp.dot(
            g_target, projection[:, c * width : (c + 1) * width], preferred_element_type=jnp.float32
        )
        target = gather_columns(cube, reduce_columns(cube, part).astype(jnp.bfloat16))
        term = jnp.dot(
            target, kernel_inv[c * width : (c + 1) * width], preferred_element_type=jnp.float32
        )
        summed = term if summed is None else summed + term
    pieces = summed.astype(jnp.bfloat16)

    for hop in reversed(range(1, cube.bits)):
        pieces = jnp.concatenate([pieces, cube.swap(pieces, hop)], axis=1)
    rest = cube.swap(pieces, 0)
    half = n // 2
    if (features // n) % 128 == 0:
        first = score_terms(projection, pieces, g_train, g_other, cube.blocks[:half], half, scale)
        second = score_terms(projection, rest, g_train, g_other, cube.blocks[half:], half, scale)
        own, other = first[0] + second[0], first[1] + second[1]
    else:
        stacked = jnp.concatenate([pieces, rest], axis=1).reshape(pieces.shape[0], n, -1)
        folded = jnp.take(stacked, jnp.argsort(cube.blocks), axis=1).reshape(pieces.shape[0], -1)
        own, other = score_terms(
            projection, folded, g_train, g_other, jnp.zeros((1,), jnp.int32), 1, scale
        )

    got = lax.ppermute(other, "ex", swap_cores)
    swapped = cube.core == 1
    value = jnp.concatenate([jnp.where(swapped, got, own), jnp.where(swapped, own, got)], axis=0)
    train = value.shape[1]
    value = value.reshape(n, -1, train)
    for hop in range(cube.bits):
        keeps, sends = [], []
        for e in range(2):
            left = sorted(cube.orders[e % cores][hop:])
            below = left.index(cube.orders[e % cores][hop])
            view = value.reshape(-1, 2, 2**below, value.shape[1], train)
            low = cube.bit[hop] == 0
            keeps.append(jnp.where(low, view[:, 0], view[:, 1]).reshape(-1, value.shape[1], train))
            sends.append(jnp.where(low, view[:, 1], view[:, 0]).reshape(-1, value.shape[1], train))
        keep = jnp.where(cube.core % 2 == 0, keeps[0], keeps[1])
        send = jnp.where(cube.core % 2 == 0, sends[0], sends[1])
        value = keep + cube.swap(send, hop)
    return value.reshape(-1, train).T


def solution(mesh):
    placed = (
        P(("groups", "ex"), "param"),
        P(("groups", "ex"), "param"),
        P("param", None),
        P("groups", "param"),
    )
    n, cores = mesh.shape["param"], mesh.shape["ex"]
    return jax.shard_map(
        lambda *args: on_device(n, cores, *args),
        mesh=mesh,
        in_specs=placed,
        out_specs=P(("groups", "ex"), "param"),
        check_vma=False,
    )
```

time: 446 us -> 233 us (0.52)
  waiting for transfers between devices: 348 us -> 84.4 us
  Pallas kernels: 0 us -> 62.7 us
  matrix products: 83.6 us -> 36.2 us
  starting transfers between devices: 0.17 us -> 24.1 us
  local copies, waits for them, and re-layouts: 0 us -> 7.72 us
  other arithmetic: 1.77 us -> 9.12 us
  between operations: 13.2 us -> 8.19 us
    reduce_scatter x3 -> x0, waiting for transfers between devices: 296 us -> none  [the longest x1 142 us: on_device(): lax.psum_scatter(train_part, 'param', scatter_dimension=1, tiled=True)]
    ppermute x0 -> x20, waiting for transfers between devices: none -> 84.4 us  [the longest x18 82.6 us: swap(): return lax.ppermute(value, BOTH, self.perms[hop])]
    pallas_call x0 -> x2, Pallas kernels: none -> 62.7 us  [score_terms(): pl.pallas_call(lambda *refs: score_kernel(parts, scale, *refs), grid_spec...]
    all_gather x2 -> x0, waiting for transfers between devices: 51.3 us -> none  [the longest x1 51.3 us: on_device(): target_full = lax.all_gather(target_feat, 'param', axis=1, tiled=True)]
    dot_general x4, matrix products: 83.6 us -> 36.2 us  [the longest x2 34.7 us: on_device(): jnp.dot(g_target, projection[:, c * width:(c + 1) * width], preferred_ele...]
    ppermute x0 -> x20, starting transfers between devices: none -> 24.1 us  [the longest x18 24.1 us: swap(): return lax.ppermute(value, BOTH, self.perms[hop])]
    slice x0 -> x8, local copies, waits for them, and re-layouts: none -> 5.85 us  [the longest x6 5.12 us: unpack(): k = message[rows, 0].astype(jnp.float32)]
    add x0 -> x7, other arithmetic: none -> 4.8 us  [the longest x4 4.43 us: reduce_columns(): value = jnp.where(low, first, second) + got]
  transfers between devices with their start and end apart: 5 -> 20, of which waited for: 4 -> 16; matrix products, arithmetic and copies ran while one was open for 12% -> 14% of each run, Pallas kernels for 0% -> 14%
where the time goes in v1:
time: 233 us
  waiting for transfers between devices  84.4 us (36%)
  Pallas kernels  62.7 us (27%)
  matrix products  36.2 us (16%)
  starting transfers between devices  24.1 us (10%)
  other arithmetic  9.12 us (4%)
  between operations  8.19 us (4%)
  local copies, waits for them, and re-layouts  7.72 us (3%)
    ppermute x18, waiting for transfers between devices, swap(): return lax.ppermute(value, BOTH, self.perms[hop])  82.6 us
    pallas_call x2, Pallas kernels, score_terms(): pl.pallas_call(lambda *refs: score_kernel(parts, scale, *refs), grid_spec...  62.7 us
    dot_general x2, matrix products, on_device(): jnp.dot(g_target, projection[:, c * width:(c + 1) * width], preferred_ele...  34.7 us
    ppermute x18, starting transfers between devices, swap(): return lax.ppermute(value, BOTH, self.perms[hop])  24.1 us
    slice x6, local copies, waits for them, and re-layouts, unpack(): k = message[rows, 0].astype(jnp.float32)  5.12 us
  transfers between devices with their start and end apart: 20, of which 16 were waited for; matrix products, arithmetic and copies ran while one was open for 14% of the time, Pallas kernels for 14%

profile of v1, /device:TPU:0, one launch (start us, length us, event | category | flops | bytes accessed | tf_op | source)
XLA Modules:
  0.0 232.5 jit_solution(137995757155989847)
XLA Ops:
  0.0 0.7 constant_dynamic-slice_fusion
  0.7 0.6 fusion.33
  2.0 16.9 %abs_reduce_fusion = (f32[]{:T(128)}, f32[256,2048]{1,0:T(8,128)S(1)}) fusion(bf16[256,8192]{1,0:T(8,128)(2,1)} %param.7, bf16[8192,4096]{1,0:T(8,128)(2,1)} %refs_4_.3), kind=kOutput, calls=%fused_computation.6 | convolution fusion | flops 8590983168 | bytes 39845892 | tf_op jit(solution)/shard_map/dot_general | solution.py:161
  19.9 3.0 %collective-permute-start.6 = (f16[272,1024]{1,0:T(8,128)(2,1)S(1)}, f16[272,1024]{1,0:T(8,128)(2,1)}, u32[]{:S(2)}, u32[]{:S(2)}) collective-permute-start(f16[272,1024]{1,0:T(8,128)(2,1)S(1)} %concatenate.73), channel_id=1, source_target_pairs={{0,2},{1,5},{2,0},{3,7},{4,6},{5,1},{6,4},{7,3},{8,10},{9,13},{10,... | collective-permute-start | bytes 1671176 | tf_op jit(solution)/shard_map/ppermute | solution.py:48
  22.9 17.9 %abs_reduce_fusion.1 = (f32[]{:T(128)}, f32[256,2048]{1,0:T(8,128)}) fusion(bf16[256,8192]{1,0:T(8,128)(2,1)} %param.7, bf16[8192,4096]{1,0:T(8,128)(2,1)} %refs_4_.3), kind=kOutput, calls=%fused_computation.9 | convolution fusion | flops 8590983168 | bytes 39845892 | tf_op jit(solution)/shard_map/dot_general | solution.py:161
  41.5 1.8 multiply_convert_fusion.1
  43.3 0.9 concatenate.64
  44.2 1.1 collective-permute-start
  46.0 1.2 slice.206
  47.9 6.2 %collective-permute-done = f16[272,1024]{1,0:T(8,128)(2,1)} collective-permute-done((f16[272,1024]{1,0:T(8,128)(2,1)}, f16[272,1024]{1,0:T(8,128)(2,1)}, u32[]{:S(2)}, u32[]{:S(2)}) %collective-permute-start) | collective-permute-done | bytes 557088 | tf_op jit(solution)/shard_map/ppermute | solution.py:48
  54.1 1.2 slice.194
  56.0 1.3 multiply_add_fusion
  57.6 1.6 collective-permute-start.7
  59.3 1.9 multiply_add_fusion.1
  61.4 0.5 collective-permute-start.1
  62.5 1.6 collective-permute-done.7
  64.2 0.5 slice.210
  65.4 2.7 %collective-permute-done.1 = f16[272,512]{1,0:T(8,128)(2,1)} collective-permute-done((f16[272,512]{1,0:T(8,128)(2,1)S(1)}, f16[272,512]{1,0:T(8,128)(2,1)}, u32[]{:S(2)}, u32[]{:S(2)}) %collective-permute-start.1) | collective-permute-done | bytes 278560 | tf_op jit(solution)/shard_map/ppermute | solution.py:48
  68.1 1.2 slice.198
  70.3 2.7 %collective-permute-start.8 = (f16[272,256]{1,0:T(8,128)(2,1)S(1)}, f16[272,256]{1,0:T(8,128)(2,1)S(1)}, u32[]{:S(2)}, u32[]{:S(2)}) collective-permute-start(f16[272,256]{1,0:T(8,128)(2,1)S(1)} %concatenate.75), channel_id=1, source_target_pairs={{0,8},{1,9},{2,10},{3,11},{4,12},{5,13},{6,14},{7,15},{8,0},{9,1},... | collective-permute-start | bytes 417800 | tf_op jit(solution)/shard_map/ppermute | solution.py:48
  73.0 1.1 multiply_add_fusion.3
  74.6 7.4 %collective-permute-done.8 = f16[272,256]{1,0:T(8,128)(2,1)S(1)} collective-permute-done((f16[272,256]{1,0:T(8,128)(2,1)S(1)}, f16[272,256]{1,0:T(8,128)(2,1)S(1)}, u32[]{:S(2)}, u32[]{:S(2)}) %collective-permute-start.8) | collective-permute-done | bytes 139296 | tf_op jit(solution)/shard_map/ppermute | solution.py:48
  82.0 0.5 slice.214
  83.4 1.6 collective-permute-done.2
  86.2 7.1 %collective-permute-done.9 = bf16[256,256]{1,0:T(8,128)(2,1)S(1)} collective-permute-done((bf16[256,256]{1,0:T(8,128)(2,1)S(1)}, bf16[256,256]{1,0:T(8,128)(2,1)S(1)}, u32[]{:S(2)}, u32[]{:S(2)}) %collective-permute-start.9) | collective-permute-done | bytes 131104 | tf_op jit(solution)/shard_map/ppermute | solution.py:48
  93.5 2.0 collective-permute-start.3
  95.6 4.0 %collective-permute-done.3 = bf16[256,256]{1,0:T(8,128)(2,1)S(1)} collective-permute-done((bf16[256,256]{1,0:T(8,128)(2,1)S(1)}, bf16[256,256]{1,0:T(8,128)(2,1)S(1)}, u32[]{:S(2)}, u32[]{:S(2)}) %collective-permute-start.3) | collective-permute-done | bytes 131104 | tf_op jit(solution)/shard_map/ppermute | solution.py:48
  99.7 2.4 %collective-permute-start.4 = (bf16[256,512]{1,0:T(8,128)(2,1)S(1)}, bf16[256,512]{1,0:T(8,128)(2,1)S(1)}, u32[]{:S(2)}, u32[]{:S(2)}) collective-permute-start(bf16[256,512]{1,0:T(8,128)(2,1)S(1)} %maximum_select_fusion.6), channel_id=1, source_target_pairs={{0,4},{1,3},{2,6},{3,1},{4,0},{5,7},{6,2},{7,5},{8,12},{9,11},{10,... | collective-permute-start | bytes 786440 | tf_op jit(solution)/shard_map/ppermute | solution.py:48
  102.2 1.3 collective-permute-start.11
  103.6 5.7 %collective-permute-done.4 = bf16[256,512]{1,0:T(8,128)(2,1)S(1)} collective-permute-done((bf16[256,512]{1,0:T(8,128)(2,1)S(1)}, bf16[256,512]{1,0:T(8,128)(2,1)S(1)}, u32[]{:S(2)}, u32[]{:S(2)}) %collective-permute-start.4) | collective-permute-done | bytes 262176 | tf_op jit(solution)/shard_map/ppermute | solution.py:48
  109.4 1.4 collective-permute-start.5
  110.8 0.7 collective-permute-done.11
  111.5 0.7 fusion.4
  112.2 6.4 %collective-permute-done.5 = bf16[256,1024]{1,0:T(8,128)(2,1)S(1)} collective-permute-done((bf16[256,1024]{1,0:T(8,128)(2,1)S(1)}, bf16[256,1024]{1,0:T(8,128)(2,1)S(1)}, u32[]{:S(2)}, u32[]{:S(2)}) %collective-permute-start.5) | collective-permute-done | bytes 524320 | tf_op jit(solution)/shard_map/ppermute | solution.py:48
  118.6 0.7 fusion.11
  119.3 2.3 collective-permute-start.12
  121.6 11.3 %collective-permute-done.12 = bf16[256,512]{1,0:T(8,128)(2,1)S(1)} collective-permute-done((bf16[256,512]{1,0:T(8,128)(2,1)S(1)}, bf16[256,512]{1,0:T(8,128)(2,1)S(1)}, u32[]{:S(2)}, u32[]{:S(2)}) %collective-permute-start.12) | collective-permute-done | bytes 262176 | tf_op jit(solution)/shard_map/ppermute | solution.py:48
  133.2 9.1 %collective-permute-done.13 = bf16[256,1024]{1,0:T(8,128)(2,1)S(1)} collective-permute-done((bf16[256,1024]{1,0:T(8,128)(2,1)S(1)}, bf16[256,1024]{1,0:T(8,128)(2,1)S(1)}, u32[]{:S(2)}, u32[]{:S(2)}) %collective-permute-start.13) | collective-permute-done | bytes 524320 | tf_op jit(solution)/shard_map/ppermute | solution.py:48
  142.8 31.4 %shard_map.64 = (f32[256,512]{1,0:T(8,128)S(1)}, f32[256,512]{1,0:T(8,128)S(1)}) custom-call(s32[4]{0:T(128)S(1)} %get-tuple-element.18.refs_0_, bf16[8192,4096]{1,0:T(8,128)(2,1)} %refs_4_.3, bf16[8192,4096]{1,0:T(8,128)(2,1)} %refs_4_.3, bf16[8192,4096]{1,0:T(8,128)(2,1)} %refs_4_.3, bf16[8192,4096]{1,0:T(8,128)(2,1)} %refs_4_.3, ...), custom_call_target="tpu_custom_call" | custom-call | flops 12884901888 | bytes 50331648 | tf_op jit(solution)/shard_map/pallas_call | solution.py:131
  174.2 31.3 %shard_map.65 = (f32[256,512]{1,0:T(8,128)S(1)}, f32[256,512]{1,0:T(8,128)S(1)}) custom-call(s32[4]{0:T(128)S(1)} %get-tuple-element.17.refs_0_, bf16[8192,4096]{1,0:T(8,128)(2,1)} %refs_4_.3, bf16[8192,4096]{1,0:T(8,128)(2,1)} %refs_4_.3, bf16[8192,4096]{1,0:T(8,128)(2,1)} %refs_4_.3, bf16[8192,4096]{1,0:T(8,128)(2,1)} %refs_4_.3, ...), custom_call_target="tpu_custom_call" | custom-call | flops 12884901888 | bytes 50331648 | tf_op jit(solution)/shard_map/pallas_call | solution.py:131
  205.7 1.9 collective-permute-done.16
  208.2 1.7 collective-permute-start.17
  209.9 7.5 %collective-permute-done.17 = f32[4,64,512]{2,1,0:T(8,128)S(1)} collective-permute-done((f32[4,64,512]{2,1,0:T(8,128)S(1)}, f32[4,64,512]{2,1,0:T(8,128)S(1)}, u32[]{:S(2)}, u32[]{:S(2)}) %collective-permute-start.17) | collective-permute-done | bytes 524320 | tf_op jit(solution)/shard_map/ppermute | solution.py:48
  217.7 0.8 collective-permute-start.18
  218.5 5.7 %collective-permute-done.18 = f32[2,64,512]{2,1,0:T(8,128)S(1)} collective-permute-done((f32[2,64,512]{2,1,0:T(8,128)S(1)}, f32[2,64,512]{2,1,0:T(8,128)S(1)}, u32[]{:S(2)}, u32[]{:S(2)}) %collective-permute-start.18) | collective-permute-done | bytes 262176 | tf_op jit(solution)/shard_map/ppermute | solution.py:48
  224.2 2.1 collective-permute-start.19
  226.4 5.5 %collective-permute-done.19 = f32[1,64,512]{2,1,0:T(8,128)S(1)} collective-permute-done((f32[1,64,512]{2,1,0:T(8,128)S(1)}, f32[1,64,512]{2,1,0:T(8,128)S(1)}, u32[]{:S(2)}, u32[]{:S(2)}) %collective-permute-start.19) | collective-permute-done | bytes 131104 | tf_op jit(solution)/shard_map/ppermute | solution.py:48
  231.8 0.7 fusion.30
  (46 shorter events, 4.4 us)
Async XLA Ops:
  19.9 26.0 %collective-permute-start.6 = (f16[272,1024]{1,0:T(8,128)(2,1)S(1)}, f16[272,1024]{1,0:T(8,128)(2,1)}, u32[]{:S(2)}, u32[]{:S(2)}) collective-permute-start(f16[272,1024]{1,0:T(8,128)(2,1)S(1)} %concatenate.73), channel_id=1, source_target_pairs={{0,2},{1,5},{2,0},{3,7},{4,6},{5,1},{6,4},{7,3},{8,10},{9,13},{10,... | collective-permute-start | bytes 1671176 | tf_op jit(solution)/shard_map/ppermute | solution.py:48
  22.9 119.8 %collective-permute-start.14 = (bf16[512,8192]{1,0:T(8,128)(2,1)}, bf16[512,8192]{1,0:T(8,128)(2,1)}, u32[]{:S(2)}, u32[]{:S(2)}) collective-permute-start(bf16[512,8192]{1,0:T(8,128)(2,1)} %refs_6_.3), channel_id=1, source_target_pairs={{0,1},{1,0},{2,3},{3,2},{4,5},{5,4},{6,7},{7,6},{8,9},{9,8},{10,11... | collective-permute-start | bytes 25165832 | tf_op jit(solution)/shard_map/ppermute | solution.py:155
  44.2 9.8 %collective-permute-start = (f16[272,1024]{1,0:T(8,128)(2,1)}, f16[272,1024]{1,0:T(8,128)(2,1)}, u32[]{:S(2)}, u32[]{:S(2)}) collective-permute-start(f16[272,1024]{1,0:T(8,128)(2,1)} %concatenate.64), channel_id=1, source_target_pairs={{0,2},{1,5},{2,0},{3,7},{4,6},{5,1},{6,4},{7,3},{8,10},{9,13},{10,... | collective-permute-start | bytes 1671176 | tf_op jit(solution)/shard_map/ppermute | solution.py:48
  57.6 6.6 %collective-permute-start.7 = (f16[272,512]{1,0:T(8,128)(2,1)S(1)}, f16[272,512]{1,0:T(8,128)(2,1)S(1)}, u32[]{:S(2)}, u32[]{:S(2)}) collective-permute-start(f16[272,512]{1,0:T(8,128)(2,1)S(1)} %concatenate.74), channel_id=1, source_target_pairs={{0,4},{1,3},{2,6},{3,1},{4,0},{5,7},{6,2},{7,5},{8,12},{9,11},{10,... | collective-permute-start | bytes 835592 | tf_op jit(solution)/shard_map/ppermute | solution.py:48
  61.4 6.7 %collective-permute-start.1 = (f16[272,512]{1,0:T(8,128)(2,1)S(1)}, f16[272,512]{1,0:T(8,128)(2,1)}, u32[]{:S(2)}, u32[]{:S(2)}) collective-permute-start(f16[272,512]{1,0:T(8,128)(2,1)S(1)} %concatenate.65), channel_id=1, source_target_pairs={{0,4},{1,3},{2,6},{3,1},{4,0},{5,7},{6,2},{7,5},{8,12},{9,11},{10,... | collective-permute-start | bytes 835592 | tf_op jit(solution)/shard_map/ppermute | solution.py:48
  70.3 11.7 %collective-permute-start.8 = (f16[272,256]{1,0:T(8,128)(2,1)S(1)}, f16[272,256]{1,0:T(8,128)(2,1)S(1)}, u32[]{:S(2)}, u32[]{:S(2)}) collective-permute-start(f16[272,256]{1,0:T(8,128)(2,1)S(1)} %concatenate.75), channel_id=1, source_target_pairs={{0,8},{1,9},{2,10},{3,11},{4,12},{5,13},{6,14},{7,15},{8,0},{9,1},... | collective-permute-start | bytes 417800 | tf_op jit(solution)/shard_map/ppermute | solution.py:48
  74.2 10.8 %collective-permute-start.2 = (f16[272,256]{1,0:T(8,128)(2,1)S(1)}, f16[272,256]{1,0:T(8,128)(2,1)S(1)}, u32[]{:S(2)}, u32[]{:S(2)}) collective-permute-start(f16[272,256]{1,0:T(8,128)(2,1)S(1)} %concatenate.66), channel_id=1, source_target_pairs={{0,8},{1,9},{2,10},{3,11},{4,12},{5,13},{6,14},{7,15},{8,0},{9,1},... | collective-permute-start | bytes 417800 | tf_op jit(solution)/shard_map/ppermute | solution.py:48
  83.2 28.3 %copy-start.1 = (bf16[4096,512]{1,0:T(8,128)(2,1)S(1)}, bf16[4096,512]{1,0:T(8,128)(2,1)}, u32[]{:S(2)}) copy-start(bf16[4096,512]{1,0:T(8,128)(2,1)} %param.9) | copy-start | bytes 12582916
  83.3 10.0 %collective-permute-start.9 = (bf16[256,256]{1,0:T(8,128)(2,1)S(1)}, bf16[256,256]{1,0:T(8,128)(2,1)S(1)}, u32[]{:S(2)}, u32[]{:S(2)}) collective-permute-start(bf16[256,256]{1,0:T(8,128)(2,1)S(1)} %add_convert_fusion), channel_id=1, source_target_pairs={{0,8},{1,9},{2,10},{3,11},{4,12},{5,13},{6,14},{7,15},{8,0},{9,1},... | collective-permute-start | bytes 393224 | tf_op jit(solution)/shard_map/ppermute | solution.py:48
  93.4 8.7 %collective-permute-start.10 = (bf16[256,512]{1,0:T(8,128)(2,1)S(1)}, bf16[256,512]{1,0:T(8,128)(2,1)S(1)}, u32[]{:S(2)}, u32[]{:S(2)}) collective-permute-start(bf16[256,512]{1,0:T(8,128)(2,1)S(1)} %maximum_select_fusion.7), channel_id=1, source_target_pairs={{0,4},{1,3},{2,6},{3,1},{4,0},{5,7},{6,2},{7,5},{8,12},{9,11},{10,... | collective-permute-start | bytes 786440 | tf_op jit(solution)/shard_map/ppermute | solution.py:48
  93.5 6.0 %collective-permute-start.3 = (bf16[256,256]{1,0:T(8,128)(2,1)S(1)}, bf16[256,256]{1,0:T(8,128)(2,1)S(1)}, u32[]{:S(2)}, u32[]{:S(2)}) collective-permute-start(bf16[256,256]{1,0:T(8,128)(2,1)S(1)} %add_convert_fusion.1), channel_id=1, source_target_pairs={{0,8},{1,9},{2,10},{3,11},{4,12},{5,13},{6,14},{7,15},{8,0},{9,1},... | collective-permute-start | bytes 393224 | tf_op jit(solution)/shard_map/ppermute | solution.py:48
  99.7 9.5 %collective-permute-start.4 = (bf16[256,512]{1,0:T(8,128)(2,1)S(1)}, bf16[256,512]{1,0:T(8,128)(2,1)S(1)}, u32[]{:S(2)}, u32[]{:S(2)}) collective-permute-start(bf16[256,512]{1,0:T(8,128)(2,1)S(1)} %maximum_select_fusion.6), channel_id=1, source_target_pairs={{0,4},{1,3},{2,6},{3,1},{4,0},{5,7},{6,2},{7,5},{8,12},{9,11},{10,... | collective-permute-start | bytes 786440 | tf_op jit(solution)/shard_map/ppermute | solution.py:48
  102.2 9.2 %collective-permute-start.11 = (bf16[256,1024]{1,0:T(8,128)(2,1)S(1)}, bf16[256,1024]{1,0:T(8,128)(2,1)S(1)}, u32[]{:S(2)}, u32[]{:S(2)}) collective-permute-start(bf16[256,1024]{1,0:T(8,128)(2,1)S(1)} %maximum_select_fusion.5), channel_id=1, source_target_pairs={{0,2},{1,5},{2,0},{3,7},{4,6},{5,1},{6,4},{7,3},{8,10},{9,13},{10,... | collective-permute-start | bytes 1572872 | tf_op jit(solution)/shard_map/ppermute | solution.py:48
  109.4 9.2 %collective-permute-start.5 = (bf16[256,1024]{1,0:T(8,128)(2,1)S(1)}, bf16[256,1024]{1,0:T(8,128)(2,1)S(1)}, u32[]{:S(2)}, u32[]{:S(2)}) collective-permute-start(bf16[256,1024]{1,0:T(8,128)(2,1)S(1)} %maximum_select_fusion.4), channel_id=1, source_target_pairs={{0,2},{1,5},{2,0},{3,7},{4,6},{5,1},{6,4},{7,3},{8,10},{9,13},{10,... | collective-permute-start | bytes 1572872 | tf_op jit(solution)/shard_map/ppermute | solution.py:48
  112.2 20.9 %copy-start = (s32[2,8]{1,0:T(2,128)S(1)}, s32[2,8]{1,0:T(2,128)}, u32[]{:S(2)}) copy-start(s32[2,8]{1,0:T(2,128)} %constant.66.clone) | copy-start | bytes 196
  119.3 13.6 %collective-permute-start.12 = (bf16[256,512]{1,0:T(8,128)(2,1)S(1)}, bf16[256,512]{1,0:T(8,128)(2,1)S(1)}, u32[]{:S(2)}, u32[]{:S(2)}) collective-permute-start(bf16[256,512]{1,0:T(8,128)(2,1)S(1)} %fusion.11), channel_id=1, source_target_pairs={{0,8},{1,9},{2,10},{3,11},{4,12},{5,13},{6,14},{7,15},{8,0},{9,1},... | collective-permute-start | bytes 786440 | tf_op jit(solution)/shard_map/ppermute | solution.py:48
  133.0 9.2 %collective-permute-start.13 = (bf16[256,1024]{1,0:T(8,128)(2,1)S(1)}, bf16[256,1024]{1,0:T(8,128)(2,1)S(1)}, u32[]{:S(2)}, u32[]{:S(2)}) collective-permute-start(bf16[256,1024]{1,0:T(8,128)(2,1)S(1)} %pad_maximum_fusion.2), channel_id=1, source_target_pairs={{0,4},{1,3},{2,6},{3,1},{4,0},{5,7},{6,2},{7,5},{8,12},{9,11},{10,... | collective-permute-start | bytes 1572872 | tf_op jit(solution)/shard_map/ppermute | solution.py:48
  142.3 31.9 %collective-permute-start.15 = (bf16[256,2048]{1,0:T(8,128)(2,1)S(1)}, bf16[256,2048]{1,0:T(8,128)(2,1)S(1)}, u32[]{:S(2)}, u32[]{:S(2)}) collective-permute-start(bf16[256,2048]{1,0:T(8,128)(2,1)S(1)} %pad_maximum_fusion.refs_5_), channel_id=1, source_target_pairs={{0,2},{1,5},{2,0},{3,7},{4,6},{5,1},{6,4},{7,3},{8,10},{9,13},{10,... | collective-permute-start | bytes 3145736 | tf_op jit(solution)/shard_map/ppermute | solution.py:48
  205.6 2.0 collective-permute-start.16
  208.2 9.2 %collective-permute-start.17 = (f32[4,64,512]{2,1,0:T(8,128)S(1)}, f32[4,64,512]{2,1,0:T(8,128)S(1)}, u32[]{:S(2)}, u32[]{:S(2)}) collective-permute-start(f32[4,64,512]{2,1,0:T(8,128)S(1)} %bitcast_select_fusion), channel_id=1, source_target_pairs={{0,2},{1,5},{2,0},{3,7},{4,6},{5,1},{6,4},{7,3},{8,10},{9,13},{10,... | collective-permute-start | bytes 1572872 | tf_op jit(solution)/shard_map/ppermute | solution.py:48
  217.7 6.4 %collective-permute-start.18 = (f32[2,64,512]{2,1,0:T(8,128)S(1)}, f32[2,64,512]{2,1,0:T(8,128)S(1)}, u32[]{:S(2)}, u32[]{:S(2)}) collective-permute-start(f32[2,64,512]{2,1,0:T(8,128)S(1)} %select_bitcast_fusion), channel_id=1, source_target_pairs={{0,4},{1,3},{2,6},{3,1},{4,0},{5,7},{6,2},{7,5},{8,12},{9,11},{10,... | collective-permute-start | bytes 786440 | tf_op jit(solution)/shard_map/ppermute | solution.py:48
  224.2 7.6 %collective-permute-start.19 = (f32[1,64,512]{2,1,0:T(8,128)S(1)}, f32[1,64,512]{2,1,0:T(8,128)S(1)}, u32[]{:S(2)}, u32[]{:S(2)}) collective-permute-start(f32[1,64,512]{2,1,0:T(8,128)S(1)} %fusion.29), channel_id=1, source_target_pairs={{0,8},{1,9},{2,10},{3,11},{4,12},{5,13},{6,14},{7,15},{8,0},{9,1},... | collective-permute-start | bytes 393224 | tf_op jit(solution)/shard_map/ppermute | solution.py:48

commit v2 on v0

v2 whole, which is shorter than its diff:
```python
import functools
import math

import jax
import jax.numpy as jnp
from jax import lax
from jax.experimental import pallas as pl
from jax.experimental.pallas import tpu as pltpu
from jax.sharding import PartitionSpec as P

BOTH = ("param", "ex")
SCALE_ROWS = 16
F32 = jnp.float32
BF16 = jnp.bfloat16


def turn(order, low):
    return order[low : 2 * low] + order[:low] + order[2 * low :]


class Cube:
    def __init__(self, n, orders):
        cores = len(orders)
        self.n, self.orders = n, orders
        self.bits = n.bit_length() - 1
        self.perms = [
            [
                (p * cores + e, (p ^ (1 << self.orders[e][h])) * cores + e)
                for p in range(n)
                for e in range(cores)
            ]
            for h in range(self.bits)
        ]
        masks = [
            [
                sum(((i >> (self.bits - 1 - h)) & 1) << self.orders[e][h] for h in range(self.bits))
                for i in range(n)
            ]
            for e in range(cores)
        ]
        self.core = lax.axis_index("ex")
        mine = jnp.array(masks, jnp.int32)[self.core]
        self.blocks = jnp.bitwise_xor(lax.axis_index("param"), mine)

    def swap(self, value, hop):
        return lax.ppermute(value, BOTH, self.perms[hop])


def product_kernel(with_top, blocks_ref, g_ref, p_ref, *refs):
    outs = refs[len(refs) - 1 - with_top :]
    value = jnp.dot(g_ref[...], p_ref[...], preferred_element_type=F32)
    outs[0][...] = value.astype(outs[0].dtype)
    if with_top:
        outs[1][...] = jnp.broadcast_to(jnp.max(jnp.abs(value), axis=0, keepdims=True), outs[1].shape)


def product(g, projection, blocks, width, dtype, with_top=False, after=()):
    rows, depth = g.shape
    count = blocks.shape[0]
    out_shape = [jax.ShapeDtypeStruct((rows, count * width), dtype)]
    out_specs = [pl.BlockSpec((rows, width), lambda i, b: (0, i))]
    if with_top:
        out_shape.append(jax.ShapeDtypeStruct((8, count * width), F32))
        out_specs.append(pl.BlockSpec((8, width), lambda i, b: (0, i)))
    return pl.pallas_call(
        functools.partial(product_kernel, with_top),
        grid_spec=pltpu.PrefetchScalarGridSpec(
            num_scalar_prefetch=1,
            grid=(count,),
            in_specs=[
                pl.BlockSpec(memory_space=pltpu.VMEM),
                pl.BlockSpec((depth, width), lambda i, b: (0, b[i])),
            ]
            + [pl.BlockSpec(memory_space=pl.ANY)] * len(after),
            out_specs=out_specs,
        ),
        out_shape=out_shape,
        compiler_params=pltpu.CompilerParams(vmem_limit_bytes=28 * 2**20),
        cost_estimate=pl.CostEstimate(
            flops=2 * rows * depth * count * width,
            bytes_accessed=2 * depth * count * width,
            transcendentals=0,
        ),
    )(blocks, g, projection, *after)


def fold_kernel(blocks_ref, target_ref, inverse_ref, out_ref):
    count = blocks_ref.shape[0]
    width = target_ref.shape[1] // count
    total = None
    for i in range(count):
        rows = pl.ds(pl.multiple_of(blocks_ref[i] * width, width), width)
        term = jnp.dot(
            target_ref[:, i * width : (i + 1) * width],
            inverse_ref[rows, :],
            preferred_element_type=F32,
        )
        total = term if total is None else total + term
    out_ref[...] = total.astype(out_ref.dtype)


def fold(target, inverse, blocks):
    rows, columns = target.shape[0], inverse.shape[1]
    vmem = pl.BlockSpec(memory_space=pltpu.VMEM)
    return pl.pallas_call(
        fold_kernel,
        in_specs=[pl.BlockSpec(memory_space=pltpu.SMEM), vmem, vmem],
        out_specs=vmem,
        out_shape=jax.ShapeDtypeStruct((rows, columns), BF16),
        compiler_params=pltpu.CompilerParams(vmem_limit_bytes=16 * 2**20),
        cost_estimate=pl.CostEstimate(
            flops=2 * rows * target.shape[1] * columns,
            bytes_accessed=2 * target.shape[1] * columns,
            transcendentals=0,
        ),
    )(blocks, target, inverse)


def score_kernel(scale, count, order_ref, own_ref, got_ref, *refs):
    train, (keep_ref, send_ref, folded_ref, placed_ref) = refs[:-4], refs[-4:]
    rows = own_ref.shape[0]
    folded_ref[:rows] = own_ref[...]
    folded_ref[rows:] = got_ref[...]
    height = 2 * rows // count
    for i in range(count):
        source = pl.ds(pl.multiple_of(order_ref[i] * height, height), height)
        placed_ref[i * height : (i + 1) * height] = folded_ref[source, :]
    folded = placed_ref[...]
    width = train[0].shape[1]
    total = None
    for c in range(len(train) // 2):
        value = train[2 * c][...] + train[2 * c + 1][...].astype(F32)
        high = value.astype(BF16)
        low = (value - high.astype(F32)).astype(BF16)
        for part in (high, low):
            term = lax.dot_general(
                folded[:, c * width : (c + 1) * width],
                part,
                (((1,), (1,)), ((), ())),
                preferred_element_type=F32,
            )
            total = term if total is None else total + term
    total = total * scale
    keep_ref[...] = total[:rows]
    send_ref[...] = total[rows:]


def score_terms(own, got, train, order, scale):
    rows, columns = own.shape
    vmem = pl.BlockSpec(memory_space=pltpu.VMEM)
    shape = jax.ShapeDtypeStruct((rows, train[0].shape[0]), F32)
    return pl.pallas_call(
        functools.partial(score_kernel, scale, order.shape[0]),
        in_specs=[pl.BlockSpec(memory_space=pltpu.SMEM)] + [vmem] * (2 + len(train)),
        out_specs=[vmem, vmem],
        out_shape=[shape, shape],
        scratch_shapes=[pltpu.VMEM((2 * rows, columns), BF16)] * 2,
        compiler_params=pltpu.CompilerParams(vmem_limit_bytes=16 * 2**20),
    )(order, own, got, *train)


def exponent(top):
    k = jnp.ceil(jnp.log2(jnp.maximum(top, 1e-37)))
    return jnp.clip(k, -110.0, 100.0)


def pack(value, k):
    tail = jnp.broadcast_to(k, (SCALE_ROWS, k.shape[1]))
    return jnp.concatenate([value * jnp.exp2(14.0 - k), tail], axis=0).astype(jnp.float16)


def unpack(message):
    rows = message.shape[0] - SCALE_ROWS
    k = message[rows:].astype(F32)[:1]
    return message[:rows].astype(F32) * jnp.exp2(k - 14.0), k


def halves(value):
    middle = value.shape[1] // 2
    return value[:, :middle], value[:, middle:]


def on_device(n, cores, g_train, g_target, projection, kernel_inv):
    plain = list(range(n.bit_length() - 1))
    low = max(1, len(plain) // 3)
    cube = Cube(n, [plain, turn(plain, low)])
    train_cube = Cube(n, [plain, plain[:low] + plain[:low - 1:-1]])
    last_cube = Cube(n, [plain, plain[low:] + plain[:low]])
    features = projection.shape[1]
    width = features // n
    scale = 1.0 / math.sqrt(features)
    swap_cores = [(e, e ^ 1) for e in range(cores)]
    half = n // 2
    chunks = 2
    pieces = [train_cube.blocks * chunks + c for c in range(chunks)]

    def train_product(c, sends, after):
        blocks = pieces[c][half:] if sends else pieces[c][:half]
        return product(g_train, projection, blocks, width // chunks, BF16, after=after)[0]

    value, top = product(g_target, projection, cube.blocks[half:], width, F32, with_top=True)
    message = pack(value, exponent(top[:1]))
    value, top = product(
        g_target, projection, cube.blocks[:half], width, F32, with_top=True, after=(value,)
    )
    k = exponent(top[:1])

    def receive(hop, value, k):
        got, other = unpack(cube.swap(message, hop))
        return value + got, jnp.maximum(k, other) + 1.0

    sends, keeps, moving = [], [], [None, None]
    value, k = receive(0, value, k)
    for hop in range(1, cube.bits):
        (keep, onward), (keep_k, onward_k) = halves(value), halves(k)
        message = pack(onward, onward_k)
        if hop == 1:
            sends.append(train_product(0, True, (value,)))
        elif hop == 2:
            sends.append(train_product(1, True, (value, sends[0])))
        value, k = keep, keep_k
        value, k = receive(hop, value, k)
    target = value.astype(BF16)
    keeps.append(train_product(0, False, (target, sends[1])))

    def train_hop(c, hop):
        if hop == 0:
            return keeps[c].astype(F32) + train_cube.swap(sends[c], 0).astype(F32)
        keep, send = halves(moving[c])
        return keep + train_cube.swap(send.astype(BF16), hop).astype(F32)

    for hop in reversed(range(cube.bits)):
        got = cube.swap(target, hop)
        target = jnp.concatenate([target, got], axis=1)
        if hop == cube.bits - 1:
            keeps.append(train_product(1, False, (target, keeps[0])))
    own = fold(target, kernel_inv, cube.blocks)
    got = lax.ppermute(own, "ex", swap_cores)

    train = []
    for c in range(chunks):
        for hop in range(cube.bits - 1):
            moving[c] = train_hop(c, hop)
        keep, send = halves(moving[c])
        train += [keep, train_cube.swap(send.astype(BF16), cube.bits - 1)]

    order = jnp.bitwise_xor(last_cube.blocks, half * cube.core)
    keep, send = score_terms(own, got, train, order, scale)
    for hop in range(cube.bits):
        value = keep + last_cube.swap(send.astype(BF16), hop).astype(F32)
        rows = value.shape[0] // 2
        keep, send = value[:rows], value[rows:]
    return value.T


def plain_on_device(g_train, g_target, projection, kernel_inv):
    factor = 1.0 / math.sqrt(projection.shape[1])
    target_part = jnp.dot(g_target, projection, preferred_element_type=F32)
    target_feat = lax.psum_scatter(target_part, "param", scatter_dimension=1, tiled=True)
    target_full = lax.all_gather(target_feat.astype(BF16), "param", axis=1, tiled=True)
    every_target = lax.all_gather(target_full, "ex", axis=0, tiled=True)
    folded = jnp.dot(every_target, kernel_inv, preferred_element_type=F32).astype(BF16)
    train_part = jnp.dot(g_train, projection, preferred_element_type=F32)
    train_feat = lax.psum_scatter(train_part, "param", scatter_dimension=1, tiled=True)
    terms = jnp.dot(train_feat, folded.astype(F32).T, precision=lax.Precision.HIGHEST)
    return lax.psum_scatter(terms * factor, "param", scatter_dimension=1, tiled=True)


def solution(mesh):
    placed = (
        P(("groups", "ex"), "param"),
        P(("groups", "ex"), "param"),
        P("param", None),
        P("groups", "param"),
    )
    n, cores = mesh.shape["param"], mesh.shape["ex"]

    def body(g_train, g_target, projection, kernel_inv):
        whole_blocks = (projection.shape[1] // n) % 256 == 0 and cores == 2 and n & (n - 1) == 0
        form = functools.partial(on_device, n, cores) if whole_blocks else plain_on_device
        return form(g_train, g_target, projection, kernel_inv)

    return jax.shard_map(
        body,
        mesh=mesh,
        in_specs=placed,
        out_specs=P(("groups", "ex"), "param"),
        check_vma=False,
    )
```

time: 446 us -> 159 us (0.36)
  waiting for transfers between devices: 348 us -> 36.3 us
  matrix products: 83.6 us -> 0 us
  Pallas kernels: 0 us -> 82.3 us
  starting transfers between devices: 0.17 us -> 31.9 us
  between operations: 13.2 us -> 0.4 us
    reduce_scatter x3 -> x0, waiting for transfers between devices: 296 us -> none  [the longest x1 142 us: on_device(): lax.psum_scatter(train_part, 'param', scatter_dimension=1, tiled=True)]
    dot_general x4 -> x0, matrix products: 83.6 us -> none  [the longest x1 46 us: on_device(): jnp.dot(g_train, projection, preferred_element_type=jnp.float32)]
    pallas_call x0 -> x8, Pallas kernels: none -> 82.3 us  [the longest x6 79.2 us: product(): pl.pallas_call(functools.partial(product_kernel, with_top), grid_spec=plt...]
    all_gather x2 -> x0, waiting for transfers between devices: 51.3 us -> none  [the longest x1 51.3 us: on_device(): target_full = lax.all_gather(target_feat, 'param', axis=1, tiled=True)]
    ppermute x0 -> x16, waiting for transfers between devices: none -> 36.3 us  [the longest x15 36.3 us: swap(): return lax.ppermute(value, BOTH, self.perms[hop])]
    ppermute x0 -> x16, starting transfers between devices: none -> 31.9 us  [the longest x15 25.2 us: swap(): return lax.ppermute(value, BOTH, self.perms[hop])]
  transfers between devices with their start and end apart: 5 -> 16, of which waited for: 4 -> 6; matrix products, arithmetic and copies ran while one was open for 12% -> 2% of each run, Pallas kernels for 0% -> 42%
where the time goes in v2:
time: 159 us
  Pallas kernels  82.3 us (52%)
  waiting for transfers between devices  36.3 us (23%)
  starting transfers between devices  31.9 us (20%)
  other arithmetic  4.76 us (3%)
  local copies, waits for them, and re-layouts  3.48 us (2%)
    pallas_call x6, Pallas kernels, product(): pl.pallas_call(functools.partial(product_kernel, with_top), grid_spec=plt...  79.2 us
    ppermute x15, waiting for transfers between devices, swap(): return lax.ppermute(value, BOTH, self.perms[hop])  36.3 us
    ppermute x15, starting transfers between devices, swap(): return lax.ppermute(value, BOTH, self.perms[hop])  25.2 us
    ppermute x1, starting transfers between devices, on_device(): got = lax.ppermute(own, 'ex', swap_cores)  6.72 us
  transfers between devices with their start and end apart: 16, of which 6 were waited for; matrix products, arithmetic and copies ran while one was open for 2% of the time, Pallas kernels for 42%

profile of v2, /device:TPU:0, one launch (start us, length us, event | category | flops | bytes accessed | tf_op | source)
XLA Modules:
  0.0 159.2 jit_solution(17306925677941700270)
XLA Ops:
  0.0 0.7 broadcast_add_fusion
  0.7 0.1 slice_bitcast_fusion.4
  0.8 2.2 %copy-done = bf16[256,8192]{1,0:T(8,128)(2,1)S(1)} copy-done((bf16[256,8192]{1,0:T(8,128)(2,1)S(1)}, bf16[256,8192]{1,0:T(8,128)(2,1)}, u32[]{:S(2)}) %copy-start) | copy-done | bytes 4194328
  3.0 14.9 %shard_map.73 = (f32[256,2048]{1,0:T(8,128)S(1)}, f32[8,2048]{1,0:T(8,128)S(1)}) custom-call(s32[4]{0:T(128)S(1)} %get-tuple-element.31.blocks_ref, bf16[256,8192]{1,0:T(8,128)(2,1)S(1)} %copy-done, bf16[8192,4096]{1,0:T(8,128)(2,1)} %p_ref.11), custom_call_target="tpu_custom_call" | custom-call | flops 8589934592 | bytes 33554432 | tf_op jit(solution)/shard_map/pallas_call | solution.py:65
  17.9 0.2 multiply_convert_fusion
  18.2 0.3 pad_maximum_fusion.1
  18.5 3.0 %collective-permute-start = (f16[272,2048]{1,0:T(8,128)(2,1)S(1)}, f16[272,2048]{1,0:T(8,128)(2,1)S(1)}, u32[]{:S(2)}, u32[]{:S(2)}) collective-permute-start(f16[272,2048]{1,0:T(8,128)(2,1)S(1)} %pad_maximum_fusion.1), channel_id=1, source_target_pairs={{0,2},{1,5},{2,0},{3,7},{4,6},{5,1},{6,4},{7,3},{8,10},{9,13},{10,... | collective-permute-start | bytes 3342344 | tf_op jit(solution)/shard_map/ppermute | solution.py:46
  21.7 15.0 %shard_map.74 = (f32[256,2048]{1,0:T(8,128)S(1)}, f32[8,2048]{1,0:T(8,128)S(1)}) custom-call(s32[4]{0:T(128)S(1)} %get-tuple-element.32.blocks_ref, bf16[256,8192]{1,0:T(8,128)(2,1)S(1)} %copy-done.1, bf16[8192,4096]{1,0:T(8,128)(2,1)} %p_ref.11, f32[256,2048]{1,0:T(8,128)S(1)} %get-tuple-element.11.refs_0_), custom_call_target="tpu_custom_call" | custom-call | flops 8589934592 | bytes 33554432 | tf_op jit(solution)/shard_map/pallas_call | solution.py:65
  36.8 0.4 multiply_add_fusion.refs_0_
  37.2 0.1 fusion
  37.3 0.1 pad_maximum_fusion.3
  37.4 1.8 %collective-permute-start.1 = (f16[272,1024]{1,0:T(8,128)(2,1)S(1)}, f16[272,1024]{1,0:T(8,128)(2,1)S(1)}, u32[]{:S(2)}, u32[]{:S(2)}) collective-permute-start(f16[272,1024]{1,0:T(8,128)(2,1)S(1)} %pad_maximum_fusion.3), channel_id=1, source_target_pairs={{0,4},{1,3},{2,6},{3,1},{4,0},{5,7},{6,2},{7,5},{8,12},{9,11},{10,... | collective-permute-start | bytes 1671176 | tf_op jit(solution)/shard_map/ppermute | solution.py:46
  39.2 12.3 %shard_map.76.refs_1_ = bf16[512,1024]{1,0:T(8,128)(2,1)S(1)} custom-call(s32[4]{0:T(128)S(1)} %get-tuple-element.30.blocks_ref, bf16[512,8192]{1,0:T(8,128)(2,1)S(1)} %bitcast.24, bf16[8192,4096]{1,0:T(8,128)(2,1)} %p_ref.11, f32[256,2048]{1,0:T(8,128)S(1)} %multiply_add_fusion.refs_0_), custom_call_target="tpu_custom_call" | custom-call | flops 8589934592 | bytes 16777216 | tf_op jit(solution)/shard_map/pallas_call | solution.py:65
  51.5 1.6 collective-permute-start.7
  53.1 0.2 slice_add_fusion.2.refs_0_
  53.5 2.7 %collective-permute-start.2 = (f16[272,512]{1,0:T(8,128)(2,1)S(1)}, f16[272,512]{1,0:T(8,128)(2,1)S(1)}, u32[]{:S(2)}, u32[]{:S(2)}) collective-permute-start(f16[272,512]{1,0:T(8,128)(2,1)S(1)} %pad_maximum_fusion.5), channel_id=1, source_target_pairs={{0,8},{1,9},{2,10},{3,11},{4,12},{5,13},{6,14},{7,15},{8,0},{9,1},... | collective-permute-start | bytes 835592 | tf_op jit(solution)/shard_map/ppermute | solution.py:46
  56.1 12.3 %shard_map.77.refs_1_ = bf16[512,1024]{1,0:T(8,128)(2,1)S(1)} custom-call(s32[4]{0:T(128)S(1)} %get-tuple-element.28.blocks_ref, bf16[512,8192]{1,0:T(8,128)(2,1)S(1)} %bitcast.24, bf16[8192,4096]{1,0:T(8,128)(2,1)} %p_ref.11, f32[256,1024]{1,0:T(8,128)S(1)} %slice_add_fusion.2.refs_0_, bf16[512,1024]{1,0:T(8,128)(2,1)S(1)} %shard_map.76.refs_1_), custom_call_target="tpu_custom_call" | custom-call | flops 8589934592 | bytes 16777216 | tf_op jit(solution)/shard_map/pallas_call | solution.py:65
  68.4 0.6 collective-permute-start.10
  69.1 0.1 fusion.2.refs_0_
  69.2 0.4 collective-permute-start.3
  69.6 12.3 %shard_map.78.refs_1_ = bf16[512,1024]{1,0:T(8,128)(2,1)S(1)} custom-call(s32[4]{0:T(128)S(1)} %get-tuple-element.29.blocks_ref, bf16[512,8192]{1,0:T(8,128)(2,1)S(1)} %bitcast.24, bf16[8192,4096]{1,0:T(8,128)(2,1)} %p_ref.11, bf16[256,512]{1,0:T(8,128)(2,1)S(1)} %fusion.2.refs_0_, bf16[512,1024]{1,0:T(8,128)(2,1)S(1)} %shard_map.77.refs_1_), custom_call_target="tpu_custom_call" | custom-call | flops 8589934592 | bytes 16777216 | tf_op jit(solution)/shard_map/pallas_call | solution.py:65
  81.9 0.4 convert_add_fusion.1
  82.3 0.1 slice.276
  82.3 2.0 %collective-permute-start.8 = (bf16[512,512]{1,0:T(8,128)(2,1)S(1)}, bf16[512,512]{1,0:T(8,128)(2,1)S(1)}, u32[]{:S(2)}, u32[]{:S(2)}) collective-permute-start(bf16[512,512]{1,0:T(8,128)(2,1)S(1)} %slice.276), channel_id=1, source_target_pairs={{0,4},{1,9},{2,6},{3,11},{4,0},{5,13},{6,2},{7,15},{8,12},{9,1},{1... | collective-permute-start | bytes 1572872 | tf_op jit(solution)/shard_map/ppermute | solution.py:46
  84.4 0.2 collective-permute-start.4
  84.6 12.5 %shard_map.79 = bf16[512,1024]{1,0:T(8,128)(2,1)S(1)} custom-call(s32[4]{0:T(128)S(1)} %get-tuple-element.27.blocks_ref, bf16[512,8192]{1,0:T(8,128)(2,1)S(1)} %bitcast.24, bf16[8192,4096]{1,0:T(8,128)(2,1)} %p_ref.11, bf16[256,1024]{1,0:T(8,128)(2,1)S(1)} %pad_maximum_fusion.4.refs_0_, bf16[512,1024]{1,0:T(8,128)(2,1)S(1)} %shard_map.78.refs_1_), custom_call_target="tpu_custom_call" | custom-call | flops 8589934592 | bytes 16777216 | tf_op jit(solution)/shard_map/pallas_call | solution.py:65
  97.0 4.1 %collective-permute-done.4 = bf16[256,1024]{1,0:T(8,128)(2,1)S(1)} collective-permute-done((bf16[256,1024]{1,0:T(8,128)(2,1)S(1)}, bf16[256,1024]{1,0:T(8,128)(2,1)S(1)}, u32[]{:S(2)}, u32[]{:S(2)}) %collective-permute-start.4) | collective-permute-done | bytes 524320 | tf_op jit(solution)/shard_map/ppermute | solution.py:46
  101.1 0.1 pad_maximum_fusion.2
  101.2 0.6 collective-permute-start.5
  101.8 0.4 convert_add_fusion
  102.2 1.8 %collective-permute-start.11 = (bf16[512,512]{1,0:T(8,128)(2,1)S(1)}, bf16[512,512]{1,0:T(8,128)(2,1)S(1)}, u32[]{:S(2)}, u32[]{:S(2)}) collective-permute-start(bf16[512,512]{1,0:T(8,128)(2,1)S(1)} %slice.275), channel_id=1, source_target_pairs={{0,4},{1,9},{2,6},{3,11},{4,0},{5,13},{6,2},{7,15},{8,12},{9,1},{1... | collective-permute-start | bytes 1572872 | tf_op jit(solution)/shard_map/ppermute | solution.py:46
  104.1 0.2 slice_add_fusion.1
  104.3 4.0 %collective-permute-start.9 = (bf16[512,256]{1,0:T(8,128)(2,1)S(1)}, bf16[512,256]{1,0:T(8,128)(2,1)S(1)}, u32[]{:S(2)}, u32[]{:S(2)}) collective-permute-start(bf16[512,256]{1,0:T(8,128)(2,1)S(1)} %slice.278), channel_id=1, source_target_pairs={{0,8},{1,5},{2,10},{3,7},{4,12},{5,1},{6,14},{7,3},{8,0},{9,13},{1... | collective-permute-start | bytes 786440 | tf_op jit(solution)/shard_map/ppermute | solution.py:46
  108.3 16.4 %collective-permute-done.11 = bf16[512,512]{1,0:T(8,128)(2,1)S(1)} collective-permute-done((bf16[512,512]{1,0:T(8,128)(2,1)S(1)}, bf16[512,512]{1,0:T(8,128)(2,1)S(1)}, u32[]{:S(2)}, u32[]{:S(2)}) %collective-permute-start.11) | collective-permute-done | bytes 524320 | tf_op jit(solution)/shard_map/ppermute | solution.py:46
  124.6 0.2 slice_add_fusion
  124.8 0.7 slice.277
  125.6 4.0 %collective-permute-start.12 = (bf16[512,256]{1,0:T(8,128)(2,1)}, bf16[512,256]{1,0:T(8,128)(2,1)S(1)}, u32[]{:S(2)}, u32[]{:S(2)}) collective-permute-start(bf16[512,256]{1,0:T(8,128)(2,1)} %slice.277), channel_id=1, source_target_pairs={{0,8},{1,5},{2,10},{3,7},{4,12},{5,1},{6,14},{7,3},{8,0},{9,13},{1... | collective-permute-start | bytes 786440 | tf_op jit(solution)/shard_map/ppermute | solution.py:46
  129.6 0.2 pad_maximum_fusion.target_ref
  129.8 1.8 %shard_map.75.own_ref = bf16[256,512]{1,0:T(8,128)(2,1)S(1)} custom-call(s32[8]{0:T(128)S(1)} %bitcast.25, bf16[256,4096]{1,0:T(8,128)(2,1)S(1)} %pad_maximum_fusion.target_ref, bf16[4096,512]{1,0:T(8,128)(2,1)S(1)} %copy-done.2), custom_call_target="tpu_custom_call" | custom-call | flops 1073741824 | bytes 4194304 | tf_op jit(solution)/shard_map/pallas_call | solution.py:105
  131.6 6.7 %collective-permute-start.6 = (bf16[256,512]{1,0:T(8,128)(2,1)S(1)}, bf16[256,512]{1,0:T(8,128)(2,1)S(1)}, u32[]{:S(2)}, u32[]{:S(2)}) collective-permute-start(bf16[256,512]{1,0:T(8,128)(2,1)S(1)} %shard_map.75.own_ref), channel_id=1, source_target_pairs={{0,1},{1,0},{2,3},{3,2},{4,5},{5,4},{6,7},{7,6},{8,9},{9,8},{10,11... | collective-permute-start | bytes 786440 | tf_op jit(solution)/shard_map/ppermute | solution.py:238
  138.4 1.4 collective-permute-done.12.refs_3_
  139.8 1.3 shard_map.80
  141.2 0.6 collective-permute-start.13
  141.8 5.8 %collective-permute-done.13 = bf16[256,512]{1,0:T(8,128)(2,1)S(1)} collective-permute-done((bf16[256,512]{1,0:T(8,128)(2,1)S(1)}, bf16[256,512]{1,0:T(8,128)(2,1)S(1)}, u32[]{:S(2)}, u32[]{:S(2)}) %collective-permute-start.13) | collective-permute-done | bytes 262176 | tf_op jit(solution)/shard_map/ppermute | solution.py:46
  147.7 2.0 %collective-permute-start.14 = (bf16[128,512]{1,0:T(8,128)(2,1)S(1)}, bf16[128,512]{1,0:T(8,128)(2,1)S(1)}, u32[]{:S(2)}, u32[]{:S(2)}) collective-permute-start(bf16[128,512]{1,0:T(8,128)(2,1)S(1)} %slice.279), channel_id=1, source_target_pairs={{0,4},{1,9},{2,6},{3,11},{4,0},{5,13},{6,2},{7,15},{8,12},{9,1},{1... | collective-permute-start | bytes 393224 | tf_op jit(solution)/shard_map/ppermute | solution.py:46
  149.7 3.5 %collective-permute-done.14 = bf16[128,512]{1,0:T(8,128)(2,1)S(1)} collective-permute-done((bf16[128,512]{1,0:T(8,128)(2,1)S(1)}, bf16[128,512]{1,0:T(8,128)(2,1)S(1)}, u32[]{:S(2)}, u32[]{:S(2)}) %collective-permute-start.14) | collective-permute-done | bytes 131104 | tf_op jit(solution)/shard_map/ppermute | solution.py:46
  153.3 5.2 %collective-permute-done.15 = bf16[64,512]{1,0:T(8,128)(2,1)S(1)} collective-permute-done((bf16[64,512]{1,0:T(8,128)(2,1)S(1)}, bf16[64,512]{1,0:T(8,128)(2,1)S(1)}, u32[]{:S(2)}, u32[]{:S(2)}) %collective-permute-start.15) | collective-permute-done | bytes 65568 | tf_op jit(solution)/shard_map/ppermute | solution.py:46
  158.5 0.7 fusion.3
  (51 shorter events, 1.0 us)
Async XLA Ops:
  0.8 2.2 %copy-start = (bf16[256,8192]{1,0:T(8,128)(2,1)S(1)}, bf16[256,8192]{1,0:T(8,128)(2,1)}, u32[]{:S(2)}) copy-start(bf16[256,8192]{1,0:T(8,128)(2,1)} %g_ref.7) | copy-start | bytes 12582916
  17.9 3.7 %copy-start.1 = (bf16[256,8192]{1,0:T(8,128)(2,1)S(1)}, bf16[256,8192]{1,0:T(8,128)(2,1)}, u32[]{:S(2)}) copy-start(bf16[256,8192]{1,0:T(8,128)(2,1)} %g_ref.7) | copy-start | bytes 12582916
  18.2 21.0 %slice-start = ((s8[8388608]{0:T(1024)(128)(4,1)}), s8[4194304]{0:T(1024)(128)(4,1)S(1)}, s32[]{:S(2)}) async-start(s8[8388608]{0:T(1024)(128)(4,1)} %bitcast.23), calls=%async_computation | async-start | bytes 8388608
  18.5 18.1 %collective-permute-start = (f16[272,2048]{1,0:T(8,128)(2,1)S(1)}, f16[272,2048]{1,0:T(8,128)(2,1)S(1)}, u32[]{:S(2)}, u32[]{:S(2)}) collective-permute-start(f16[272,2048]{1,0:T(8,128)(2,1)S(1)} %pad_maximum_fusion.1), channel_id=1, source_target_pairs={{0,2},{1,5},{2,0},{3,7},{4,6},{5,1},{6,4},{7,3},{8,10},{9,13},{10,... | collective-permute-start | bytes 3342344 | tf_op jit(solution)/shard_map/ppermute | solution.py:46
  21.7 17.5 %slice-start.1 = ((s8[8388608]{0:T(1024)(128)(4,1)}), s8[4194304]{0:T(1024)(128)(4,1)S(1)}, s32[]{:S(2)}) async-start(s8[8388608]{0:T(1024)(128)(4,1)} %bitcast.23), calls=%async_computation.1 | async-start | bytes 8388608
  37.4 15.6 %collective-permute-start.1 = (f16[272,1024]{1,0:T(8,128)(2,1)S(1)}, f16[272,1024]{1,0:T(8,128)(2,1)S(1)}, u32[]{:S(2)}, u32[]{:S(2)}) collective-permute-start(f16[272,1024]{1,0:T(8,128)(2,1)S(1)} %pad_maximum_fusion.3), channel_id=1, source_target_pairs={{0,4},{1,3},{2,6},{3,1},{4,0},{5,7},{6,2},{7,5},{8,12},{9,11},{10,... | collective-permute-start | bytes 1671176 | tf_op jit(solution)/shard_map/ppermute | solution.py:46
  51.5 30.4 %collective-permute-start.7 = (bf16[512,1024]{1,0:T(8,128)(2,1)S(1)}, bf16[512,1024]{1,0:T(8,128)(2,1)S(1)}, u32[]{:S(2)}, u32[]{:S(2)}) collective-permute-start(bf16[512,1024]{1,0:T(8,128)(2,1)S(1)} %shard_map.76.refs_1_), channel_id=1, source_target_pairs={{0,2},{1,3},{2,0},{3,1},{4,6},{5,7},{6,4},{7,5},{8,10},{9,11},{10,... | collective-permute-start | bytes 3145736 | tf_op jit(solution)/shard_map/ppermute | solution.py:46
  53.5 15.5 %collective-permute-start.2 = (f16[272,512]{1,0:T(8,128)(2,1)S(1)}, f16[272,512]{1,0:T(8,128)(2,1)S(1)}, u32[]{:S(2)}, u32[]{:S(2)}) collective-permute-start(f16[272,512]{1,0:T(8,128)(2,1)S(1)} %pad_maximum_fusion.5), channel_id=1, source_target_pairs={{0,8},{1,9},{2,10},{3,11},{4,12},{5,13},{6,14},{7,15},{8,0},{9,1},... | collective-permute-start | bytes 835592 | tf_op jit(solution)/shard_map/ppermute | solution.py:46
  68.4 33.3 %collective-permute-start.10 = (bf16[512,1024]{1,0:T(8,128)(2,1)S(1)}, bf16[512,1024]{1,0:T(8,128)(2,1)S(1)}, u32[]{:S(2)}, u32[]{:S(2)}) collective-permute-start(bf16[512,1024]{1,0:T(8,128)(2,1)S(1)} %shard_map.77.refs_1_), channel_id=1, source_target_pairs={{0,2},{1,3},{2,0},{3,1},{4,6},{5,7},{6,4},{7,5},{8,10},{9,11},{10,... | collective-permute-start | bytes 3145736 | tf_op jit(solution)/shard_map/ppermute | solution.py:46
  69.2 15.1 %collective-permute-start.3 = (bf16[256,512]{1,0:T(8,128)(2,1)S(1)}, bf16[256,512]{1,0:T(8,128)(2,1)S(1)}, u32[]{:S(2)}, u32[]{:S(2)}) collective-permute-start(bf16[256,512]{1,0:T(8,128)(2,1)S(1)} %fusion.2.refs_0_), channel_id=1, source_target_pairs={{0,8},{1,9},{2,10},{3,11},{4,12},{5,13},{6,14},{7,15},{8,0},{9,1},... | collective-permute-start | bytes 786440 | tf_op jit(solution)/shard_map/ppermute | solution.py:46
  82.3 21.7 %collective-permute-start.8 = (bf16[512,512]{1,0:T(8,128)(2,1)S(1)}, bf16[512,512]{1,0:T(8,128)(2,1)S(1)}, u32[]{:S(2)}, u32[]{:S(2)}) collective-permute-start(bf16[512,512]{1,0:T(8,128)(2,1)S(1)} %slice.276), channel_id=1, source_target_pairs={{0,4},{1,9},{2,6},{3,11},{4,0},{5,13},{6,2},{7,15},{8,12},{9,1},{1... | collective-permute-start | bytes 1572872 | tf_op jit(solution)/shard_map/ppermute | solution.py:46
  84.4 16.8 %collective-permute-start.4 = (bf16[256,1024]{1,0:T(8,128)(2,1)S(1)}, bf16[256,1024]{1,0:T(8,128)(2,1)S(1)}, u32[]{:S(2)}, u32[]{:S(2)}) collective-permute-start(bf16[256,1024]{1,0:T(8,128)(2,1)S(1)} %pad_maximum_fusion.4.refs_0_), channel_id=1, source_target_pairs={{0,4},{1,3},{2,6},{3,1},{4,0},{5,7},{6,2},{7,5},{8,12},{9,11},{10,... | collective-permute-start | bytes 1572872 | tf_op jit(solution)/shard_map/ppermute | solution.py:46
  101.2 28.4 %collective-permute-start.5 = (bf16[256,2048]{1,0:T(8,128)(2,1)S(1)}, bf16[256,2048]{1,0:T(8,128)(2,1)S(1)}, u32[]{:S(2)}, u32[]{:S(2)}) collective-permute-start(bf16[256,2048]{1,0:T(8,128)(2,1)S(1)} %pad_maximum_fusion.2), channel_id=1, source_target_pairs={{0,2},{1,5},{2,0},{3,7},{4,6},{5,1},{6,4},{7,3},{8,10},{9,13},{10,... | collective-permute-start | bytes 3145736 | tf_op jit(solution)/shard_map/ppermute | solution.py:46
  102.2 22.4 %collective-permute-start.11 = (bf16[512,512]{1,0:T(8,128)(2,1)S(1)}, bf16[512,512]{1,0:T(8,128)(2,1)S(1)}, u32[]{:S(2)}, u32[]{:S(2)}) collective-permute-start(bf16[512,512]{1,0:T(8,128)(2,1)S(1)} %slice.275), channel_id=1, source_target_pairs={{0,4},{1,9},{2,6},{3,11},{4,0},{5,13},{6,2},{7,15},{8,12},{9,1},{1... | collective-permute-start | bytes 1572872 | tf_op jit(solution)/shard_map/ppermute | solution.py:46
  104.3 34.1 %collective-permute-start.9 = (bf16[512,256]{1,0:T(8,128)(2,1)S(1)}, bf16[512,256]{1,0:T(8,128)(2,1)S(1)}, u32[]{:S(2)}, u32[]{:S(2)}) collective-permute-start(bf16[512,256]{1,0:T(8,128)(2,1)S(1)} %slice.278), channel_id=1, source_target_pairs={{0,8},{1,5},{2,10},{3,7},{4,12},{5,1},{6,14},{7,3},{8,0},{9,13},{1... | collective-permute-start | bytes 786440 | tf_op jit(solution)/shard_map/ppermute | solution.py:46
  125.6 4.2 %copy-start.2 = (bf16[4096,512]{1,0:T(8,128)(2,1)S(1)}, bf16[4096,512]{1,0:T(8,128)(2,1)}, u32[]{:S(2)}) copy-start(bf16[4096,512]{1,0:T(8,128)(2,1)} %inverse_ref.1) | copy-start | bytes 12582916
  125.6 14.2 %collective-permute-start.12 = (bf16[512,256]{1,0:T(8,128)(2,1)}, bf16[512,256]{1,0:T(8,128)(2,1)S(1)}, u32[]{:S(2)}, u32[]{:S(2)}) collective-permute-start(bf16[512,256]{1,0:T(8,128)(2,1)} %slice.277), channel_id=1, source_target_pairs={{0,8},{1,5},{2,10},{3,7},{4,12},{5,1},{6,14},{7,3},{8,0},{9,13},{1... | collective-permute-start | bytes 786440 | tf_op jit(solution)/shard_map/ppermute | solution.py:46
  129.8 8.5 %copy-start.3 = (s32[2,8]{1,0:T(2,128)S(1)}, s32[2,8]{1,0:T(2,128)}, u32[]{:S(2)}) copy-start(s32[2,8]{1,0:T(2,128)} %constant.48.clone) | copy-start | bytes 196
  131.6 8.2 %collective-permute-start.6 = (bf16[256,512]{1,0:T(8,128)(2,1)S(1)}, bf16[256,512]{1,0:T(8,128)(2,1)S(1)}, u32[]{:S(2)}, u32[]{:S(2)}) collective-permute-start(bf16[256,512]{1,0:T(8,128)(2,1)S(1)} %shard_map.75.own_ref), channel_id=1, source_target_pairs={{0,1},{1,0},{2,3},{3,2},{4,5},{5,4},{6,7},{7,6},{8,9},{9,8},{10,11... | collective-permute-start | bytes 786440 | tf_op jit(solution)/shard_map/ppermute | solution.py:238
  141.2 6.4 %collective-permute-start.13 = (bf16[256,512]{1,0:T(8,128)(2,1)S(1)}, bf16[256,512]{1,0:T(8,128)(2,1)S(1)}, u32[]{:S(2)}, u32[]{:S(2)}) collective-permute-start(bf16[256,512]{1,0:T(8,128)(2,1)S(1)} %convert_element_type.64), channel_id=1, source_target_pairs={{0,2},{1,5},{2,0},{3,7},{4,6},{5,1},{6,4},{7,3},{8,10},{9,13},{10,... | collective-permute-start | bytes 786440 | tf_op jit(solution)/shard_map/ppermute | solution.py:46
  147.7 5.5 %collective-permute-start.14 = (bf16[128,512]{1,0:T(8,128)(2,1)S(1)}, bf16[128,512]{1,0:T(8,128)(2,1)S(1)}, u32[]{:S(2)}, u32[]{:S(2)}) collective-permute-start(bf16[128,512]{1,0:T(8,128)(2,1)S(1)} %slice.279), channel_id=1, source_target_pairs={{0,4},{1,9},{2,6},{3,11},{4,0},{5,13},{6,2},{7,15},{8,12},{9,1},{1... | collective-permute-start | bytes 393224 | tf_op jit(solution)/shard_map/ppermute | solution.py:46
  153.3 5.2 %collective-permute-start.15 = (bf16[64,512]{1,0:T(8,128)(2,1)S(1)}, bf16[64,512]{1,0:T(8,128)(2,1)S(1)}, u32[]{:S(2)}, u32[]{:S(2)}) collective-permute-start(bf16[64,512]{1,0:T(8,128)(2,1)S(1)} %slice.280), channel_id=1, source_target_pairs={{0,8},{1,3},{2,10},{3,1},{4,12},{5,7},{6,14},{7,5},{8,0},{9,11},{1... | collective-permute-start | bytes 196616 | tf_op jit(solution)/shard_map/ppermute | solution.py:46

commit v3 on v2

--- a/solution.py
+++ b/solution.py
@@ -12,10 +12,7 @@
 SCALE_ROWS = 16
 F32 = jnp.float32
 BF16 = jnp.bfloat16
-
-
-def turn(order, low):
-    return order[low : 2 * low] + order[:low] + order[2 * low :]
+LIGHT = pl.CostEstimate(flops=1024, bytes_accessed=1024, transcendentals=0)
 
 
 class Cube:
@@ -31,7 +28,7 @@
             ]
             for h in range(self.bits)
         ]
-        masks = [
+        self.masks = [
             [
                 sum(((i >> (self.bits - 1 - h)) & 1) << self.orders[e][h] for h in range(self.bits))
                 for i in range(n)
@@ -39,8 +36,11 @@
             for e in range(cores)
         ]
         self.core = lax.axis_index("ex")
-        mine = jnp.array(masks, jnp.int32)[self.core]
+        mine = jnp.array(self.masks, jnp.int32)[self.core]
         self.blocks = jnp.bitwise_xor(lax.axis_index("param"), mine)
+
+    def partners(self, e, i):
+        return [p ^ self.masks[e][i] for p in range(self.n)]
 
     def swap(self, value, hop):
         return lax.ppermute(value, BOTH, self.perms[hop])
@@ -76,11 +76,7 @@
         ),
         out_shape=out_shape,
         compiler_params=pltpu.CompilerParams(vmem_limit_bytes=28 * 2**20),
-        cost_estimate=pl.CostEstimate(
-            flops=2 * rows * depth * count * width,
-            bytes_accessed=2 * depth * count * width,
-            transcendentals=0,
-        ),
+        cost_estimate=LIGHT,
     )(blocks, g, projection, *after)
 
 
@@ -108,16 +104,12 @@
         out_specs=vmem,
         out_shape=jax.ShapeDtypeStruct((rows, columns), BF16),
         compiler_params=pltpu.CompilerParams(vmem_limit_bytes=16 * 2**20),
-        cost_estimate=pl.CostEstimate(
-            flops=2 * rows * target.shape[1] * columns,
-            bytes_accessed=2 * target.shape[1] * columns,
-            transcendentals=0,
-        ),
+        cost_estimate=LIGHT,
     )(blocks, target, inverse)
 
 
 def score_kernel(scale, count, order_ref, own_ref, got_ref, *refs):
-    train, (keep_ref, send_ref, folded_ref, placed_ref) = refs[:-4], refs[-4:]
+    train, outs, (folded_ref, placed_ref) = refs[: -2 - count], refs[-2 - count : -2], refs[-2:]
     rows = own_ref.shape[0]
     folded_ref[:rows] = own_ref[...]
     folded_ref[rows:] = got_ref[...]
@@ -141,20 +133,22 @@
             )
             total = term if total is None else total + term
     total = total * scale
-    keep_ref[...] = total[:rows]
-    send_ref[...] = total[rows:]
+    for i in range(count):
+        outs[i][...] = total[i * height : (i + 1) * height].astype(outs[i].dtype)
 
 
 def score_terms(own, got, train, order, scale):
     rows, columns = own.shape
+    count = order.shape[0]
     vmem = pl.BlockSpec(memory_space=pltpu.VMEM)
-    shape = jax.ShapeDtypeStruct((rows, train[0].shape[0]), F32)
+    shape = (2 * rows // count, train[0].shape[0])
     return pl.pallas_call(
-        functools.partial(score_kernel, scale, order.shape[0]),
+        functools.partial(score_kernel, scale, count),
         in_specs=[pl.BlockSpec(memory_space=pltpu.SMEM)] + [vmem] * (2 + len(train)),
-        out_specs=[vmem, vmem],
-        out_shape=[shape, shape],
+        out_specs=[vmem] * count,
+        out_shape=[jax.ShapeDtypeStruct(shape, BF16 if i else F32) for i in range(count)],
         scratch_shapes=[pltpu.VMEM((2 * rows, columns), BF16)] * 2,
+        cost_estimate=LIGHT,
         compiler_params=pltpu.CompilerParams(vmem_limit_bytes=16 * 2**20),
     )(order, own, got, *train)
 
@@ -180,76 +174,109 @@
     return value[:, :middle], value[:, middle:]
 
 
+STEPS = (
+    "TS", "sT0", "TK", "dT0", "sT1", "Sb", "dT1", "sT2", "sB0", "Kb", "dT2", "sG0", "dB0", "sB1", "Sa", "sA0", "dG0", "sG1", "Ka", "dB1", "dG1", "sG2", "dA0", "sA1", "sB2", "dA1", "sA2", "dG2", "F", "sE0", "dE0", "dB2", "dA2", "SC",
+)
+AXES = {"T": ("lxh", "xhl"), "L": ("xlh", "lxh"), "A": ("lxh", "xhl"), "B": ("xhl", "lxh")}
+
+
 def on_device(n, cores, g_train, g_target, projection, kernel_inv):
-    plain = list(range(n.bit_length() - 1))
-    low = max(1, len(plain) // 3)
-    cube = Cube(n, [plain, turn(plain, low)])
-    train_cube = Cube(n, [plain, plain[:low] + plain[:low - 1:-1]])
-    last_cube = Cube(n, [plain, plain[low:] + plain[:low]])
     features = projection.shape[1]
     width = features // n
     scale = 1.0 / math.sqrt(features)
     swap_cores = [(e, e ^ 1) for e in range(cores)]
     half = n // 2
-    chunks = 2
-    pieces = [train_cube.blocks * chunks + c for c in range(chunks)]
-
-    def train_product(c, sends, after):
-        blocks = pieces[c][half:] if sends else pieces[c][:half]
-        return product(g_train, projection, blocks, width // chunks, BF16, after=after)[0]
-
-    value, top = product(g_target, projection, cube.blocks[half:], width, F32, with_top=True)
-    message = pack(value, exponent(top[:1]))
-    value, top = product(
-        g_target, projection, cube.blocks[:half], width, F32, with_top=True, after=(value,)
-    )
-    k = exponent(top[:1])
-
-    def receive(hop, value, k):
-        got, other = unpack(cube.swap(message, hop))
-        return value + got, jnp.maximum(k, other) + 1.0
-
-    sends, keeps, moving = [], [], [None, None]
-    value, k = receive(0, value, k)
-    for hop in range(1, cube.bits):
-        (keep, onward), (keep_k, onward_k) = halves(value), halves(k)
-        message = pack(onward, onward_k)
-        if hop == 1:
-            sends.append(train_product(0, True, (value,)))
-        elif hop == 2:
-            sends.append(train_product(1, True, (value, sends[0])))
-        value, k = keep, keep_k
-        value, k = receive(hop, value, k)
-    target = value.astype(BF16)
-    keeps.append(train_product(0, False, (target, sends[1])))
-
-    def train_hop(c, hop):
-        if hop == 0:
-            return keeps[c].astype(F32) + train_cube.swap(sends[c], 0).astype(F32)
-        keep, send = halves(moving[c])
-        return keep + train_cube.swap(send.astype(BF16), hop).astype(F32)
-
-    for hop in reversed(range(cube.bits)):
-        got = cube.swap(target, hop)
-        target = jnp.concatenate([target, got], axis=1)
-        if hop == cube.bits - 1:
-            keeps.append(train_product(1, False, (target, keeps[0])))
-    own = fold(target, kernel_inv, cube.blocks)
-    got = lax.ppermute(own, "ex", swap_cores)
-
-    train = []
-    for c in range(chunks):
-        for hop in range(cube.bits - 1):
-            moving[c] = train_hop(c, hop)
-        keep, send = halves(moving[c])
-        train += [keep, train_cube.swap(send.astype(BF16), cube.bits - 1)]
-
-    order = jnp.bitwise_xor(last_cube.blocks, half * cube.core)
-    keep, send = score_terms(own, got, train, order, scale)
-    for hop in range(cube.bits):
-        value = keep + last_cube.swap(send.astype(BF16), hop).astype(F32)
-        rows = value.shape[0] // 2
-        keep, send = value[:rows], value[rows:]
+    cubes = {unit: Cube(n, [["xlh".index(c) for c in axes] for axes in AXES[unit]]) for unit in AXES}
+    hops = cubes["T"].bits
+    last = []
+
+    def ordered(*values):
+        return lax.optimization_barrier((*values, *last))[: len(values)]
+
+    def done(value):
+        last[:] = [value]
+        return value
+
+    made, moving = {}, {}
+
+    def run(step):
+        kind, unit = step[0], step[1:2].upper()
+        hop = int(step[2]) if len(step) == 3 else None
+        if step in ("TS", "TK"):
+            cube = cubes["T"]
+            (blocks,) = ordered(cube.blocks[half:] if step == "TS" else cube.blocks[:half])
+            value, top = product(g_target, projection, blocks, width, F32, with_top=True)
+            made[step] = done(value), exponent(top[:1])
+        elif step in ("Sa", "Ka", "Sb", "Kb"):
+            blocks = cubes[unit].blocks * 2 + "AB".index(unit)
+            blocks, dtype = (blocks[half:], BF16) if kind == "S" else (blocks[:half], F32)
+            (blocks,) = ordered(blocks)
+            made[step] = done(product(g_train, projection, blocks, width // 2, dtype)[0])
+        elif step == "F":
+            (target,) = ordered(moving["G"])
+            made["F"] = done(fold(target, kernel_inv, cubes["T"].blocks))
+        elif step == "SC":
+            order = jnp.bitwise_xor(cubes["L"].blocks, half * cubes["L"].core)
+            (order,) = ordered(order)
+            train = [term for part in "AB" for term in moving[part]]
+            made["SC"] = score_terms(made["F"], moving["E"], train, order, scale)
+        elif unit == "T" and kind == "s":
+            if hop == 0:
+                kept, (value, k) = None, made["TS"]
+            else:
+                (keep, value), (keep_k, k) = map(halves, moving["T"])
+                kept = keep, keep_k
+            (value,) = ordered(value)
+            message = done(pack(value, k))
+            moving["T"] = kept, cubes["T"].swap(message, hop)
+        elif unit == "T":
+            kept, got = moving["T"]
+            value, k = made["TK"] if hop == 0 else kept
+            (got,) = ordered(got)
+            got, other = unpack(got)
+            moving["T"] = done(value + got), jnp.maximum(k, other) + 1.0
+            if hop == hops - 1:
+                moving["G"] = done(moving["T"][0].astype(BF16))
+        elif unit == "G" and kind == "s":
+            (value,) = ordered(moving["G"])
+            moving["G"] = value, cubes["T"].swap(done(value), hops - 1 - hop)
+        elif unit == "G":
+            value, got = moving["G"]
+            (got,) = ordered(got)
+            moving["G"] = done(jnp.concatenate([value, got], axis=1))
+        elif unit == "E" and kind == "s":
+            moving["E"] = lax.ppermute(made["F"], "ex", swap_cores)
+        elif unit == "E":
+            pass
+        elif kind == "s":
+            if hop == 0:
+                keep, send = None, made["S" + unit.lower()]
+            else:
+                keep, send = halves(moving[unit])
+            (send,) = ordered(send)
+            send = done(send.astype(BF16))
+            moving[unit] = keep, cubes[unit].swap(send, hop)
+        else:
+            keep, got = moving[unit]
+            keep = made["K" + unit.lower()] if hop == 0 else keep
+            (got,) = ordered(got)
+            if hop == hops - 1:
+                moving[unit] = keep, got
+            else:
+                moving[unit] = done(keep + got.astype(F32))
+
+    for step in STEPS:
+        run(step)
+
+    parts = made["SC"]
+    value = parts[0]
+    for i in range(1, n):
+        pairs = [
+            (p * cores + e, p_to * cores + e)
+            for e in range(cores)
+            for p, p_to in enumerate(cubes["L"].partners(e, i))
+        ]
+        value = value + lax.ppermute(parts[i], BOTH, pairs).astype(F32)
     return value.T
 
 
@@ -276,7 +303,7 @@
     n, cores = mesh.shape["param"], mesh.shape["ex"]
 
     def body(g_train, g_target, projection, kernel_inv):
-        whole_blocks = (projection.shape[1] // n) % 256 == 0 and cores == 2 and n & (n - 1) == 0
+        whole_blocks = n == 8 and cores == 2 and (projection.shape[1] // n) % 256 == 0
         form = functools.partial(on_device, n, cores) if whole_blocks else plain_on_device
         return form(g_train, g_target, projection, kernel_inv)
 

time: 159 us -> 152 us (0.956)
  waiting for transfers between devices: 36.3 us -> 29.1 us
    ppermute x15 -> x12, waiting for transfers between devices: 36.3 us -> 23.7 us  [swap(): return lax.ppermute(value, BOTH, self.perms[hop])]
    ppermute x15 -> x12, starting transfers between devices: 25.2 us -> 17.9 us  [swap(): return lax.ppermute(value, BOTH, self.perms[hop])]
    ppermute x1 -> x8, starting transfers between devices: 6.72 us -> 13.7 us  [the longest x7 9.72 us: on_device(): value = value + lax.ppermute(parts[i], BOTH, pairs).astype(F32)]
    ppermute x1 -> x8, waiting for transfers between devices: 0.01 us -> 5.37 us  [the longest x7 5.37 us: on_device(): value = value + lax.ppermute(parts[i], BOTH, pairs).astype(F32)]
  transfers between devices with their start and end apart: 16 -> 20, of which waited for: 6 -> 8; matrix products, arithmetic and copies ran while one was open for 2% -> 2% of each run, Pallas kernels for 42% -> 44%
where the time goes in v3:
time: 152 us
  Pallas kernels  82.4 us (54%)
  starting transfers between devices  31.6 us (21%)
  waiting for transfers between devices  29.1 us (19%)
  other arithmetic  4.73 us (3%)
  local copies, waits for them, and re-layouts  3.59 us (2%)
    pallas_call x6, Pallas kernels, product(): pl.pallas_call(functools.partial(product_kernel, with_top), grid_spec=plt...  79.2 us
    ppermute x12, waiting for transfers between devices, swap(): return lax.ppermute(value, BOTH, self.perms[hop])  23.7 us
    ppermute x12, starting transfers between devices, swap(): return lax.ppermute(value, BOTH, self.perms[hop])  17.9 us
    ppermute x7, starting transfers between devices, on_device(): value = value + lax.ppermute(parts[i], BOTH, pairs).astype(F32)  9.72 us
    ppermute x7, waiting for transfers between devices, on_device(): value = value + lax.ppermute(parts[i], BOTH, pairs).astype(F32)  5.37 us
    ppermute x1, starting transfers between devices, run(): moving['E'] = lax.ppermute(made['F'], 'ex', swap_cores)  3.94 us
  transfers between devices with their start and end apart: 20, of which 8 were waited for; matrix products, arithmetic and copies ran while one was open for 2% of the time, Pallas kernels for 44%

profile of v3, /device:TPU:0, one launch (start us, length us, event | category | flops | bytes accessed | tf_op | source)
XLA Modules:
  0.0 151.8 jit_solution(1368864605870865795)
XLA Ops:
  0.0 0.7 broadcast_multiply_fusion
  0.8 2.2 %copy-done = bf16[256,8192]{1,0:T(8,128)(2,1)S(1)} copy-done((bf16[256,8192]{1,0:T(8,128)(2,1)S(1)}, bf16[256,8192]{1,0:T(8,128)(2,1)}, u32[]{:S(2)}) %copy-start) | copy-done | bytes 4194328
  3.0 14.7 %shard_map.82 = (f32[256,2048]{1,0:T(8,128)S(1)}, f32[8,2048]{1,0:T(8,128)S(1)}) custom-call(s32[4]{0:T(128)S(1)} %get-tuple-element.93.blocks_ref, bf16[256,8192]{1,0:T(8,128)(2,1)S(1)} %copy-done, bf16[8192,4096]{1,0:T(8,128)(2,1)} %p_ref.11), custom_call_target="tpu_custom_call" | custom-call | flops 1024 | bytes 1024 | tf_op jit(solution)/shard_map/pallas_call | solution.py:65
  17.8 0.2 multiply_convert_fusion
  18.0 0.3 pad_maximum_fusion.1
  18.3 3.1 %collective-permute-start = (f16[272,2048]{1,0:T(8,128)(2,1)S(1)}, f16[272,2048]{1,0:T(8,128)(2,1)S(1)}, u32[]{:S(2)}, u32[]{:S(2)}) collective-permute-start(f16[272,2048]{1,0:T(8,128)(2,1)S(1)} %pad_maximum_fusion.1), channel_id=1, source_target_pairs={{0,4},{1,3},{2,6},{3,1},{4,0},{5,7},{6,2},{7,5},{8,12},{9,11},{10,... | collective-permute-start | bytes 3342344 | tf_op jit(solution)/shard_map/ppermute | solution.py:46
  21.4 15.2 %shard_map.83 = (f32[256,2048]{1,0:T(8,128)S(1)}, f32[8,2048]{1,0:T(8,128)S(1)}) custom-call(s32[4]{0:T(128)S(1)} %get-tuple-element.44.blocks_ref, bf16[256,8192]{1,0:T(8,128)(2,1)S(1)} %copy-done.1, bf16[8192,4096]{1,0:T(8,128)(2,1)} %p_ref.11), custom_call_target="tpu_custom_call" | custom-call | flops 1024 | bytes 1024 | tf_op jit(solution)/shard_map/pallas_call | solution.py:65
  36.7 0.4 multiply_add_fusion
  37.1 0.1 slice.159
  37.2 0.1 multiply_convert_fusion.1
  37.3 0.1 pad_maximum_fusion.3
  37.5 1.8 %collective-permute-start.1 = (f16[272,1024]{1,0:T(8,128)(2,1)S(1)}, f16[272,1024]{1,0:T(8,128)(2,1)S(1)}, u32[]{:S(2)}, u32[]{:S(2)}) collective-permute-start(f16[272,1024]{1,0:T(8,128)(2,1)S(1)} %pad_maximum_fusion.3), channel_id=1, source_target_pairs={{0,2},{1,9},{2,0},{3,11},{4,6},{5,13},{6,4},{7,15},{8,10},{9,1},{1... | collective-permute-start | bytes 1671176 | tf_op jit(solution)/shard_map/ppermute | solution.py:46
  39.3 12.3 %shard_map.84 = bf16[512,1024]{1,0:T(8,128)(2,1)S(1)} custom-call(s32[4]{0:T(128)S(1)} %get-tuple-element.49.blocks_ref, bf16[512,8192]{1,0:T(8,128)(2,1)S(1)} %bitcast.24, bf16[8192,4096]{1,0:T(8,128)(2,1)} %p_ref.11), custom_call_target="tpu_custom_call" | custom-call | flops 1024 | bytes 1024 | tf_op jit(solution)/shard_map/pallas_call | solution.py:65
  51.6 0.2 slice_add_fusion.2
  52.0 0.4 collective-permute-start.4
  52.4 2.8 %collective-permute-start.2 = (f16[272,512]{1,0:T(8,128)(2,1)S(1)}, f16[272,512]{1,0:T(8,128)(2,1)S(1)}, u32[]{:S(2)}, u32[]{:S(2)}) collective-permute-start(f16[272,512]{1,0:T(8,128)(2,1)S(1)} %pad_maximum_fusion.5), channel_id=1, source_target_pairs={{0,8},{1,5},{2,10},{3,7},{4,12},{5,1},{6,14},{7,3},{8,0},{9,13},{1... | collective-permute-start | bytes 835592 | tf_op jit(solution)/shard_map/ppermute | solution.py:46
  55.2 12.3 %shard_map.85 = f32[512,1024]{1,0:T(8,128)S(1)} custom-call(s32[4]{0:T(128)S(1)} %get-tuple-element.53.blocks_ref, bf16[512,8192]{1,0:T(8,128)(2,1)S(1)} %bitcast.24, bf16[8192,4096]{1,0:T(8,128)(2,1)} %p_ref.11), custom_call_target="tpu_custom_call" | custom-call | flops 1024 | bytes 1024 | tf_op jit(solution)/shard_map/pallas_call | solution.py:65
  67.7 0.2 collective-permute-start.3
  67.9 0.4 convert_add_fusion.1
  68.4 2.8 %collective-permute-start.6 = (bf16[512,512]{1,0:T(8,128)(2,1)S(1)}, bf16[512,512]{1,0:T(8,128)(2,1)S(1)}, u32[]{:S(2)}, u32[]{:S(2)}) collective-permute-start(bf16[512,512]{1,0:T(8,128)(2,1)S(1)} %slice.166), channel_id=1, source_target_pairs={{0,8},{1,3},{2,10},{3,1},{4,12},{5,7},{6,14},{7,5},{8,0},{9,11},{1... | collective-permute-start | bytes 1572872 | tf_op jit(solution)/shard_map/ppermute | solution.py:46
  71.3 12.3 %shard_map.86 = bf16[512,1024]{1,0:T(8,128)(2,1)S(1)} custom-call(s32[4]{0:T(128)S(1)} %get-tuple-element.57.blocks_ref, bf16[512,8192]{1,0:T(8,128)(2,1)S(1)} %bitcast.24, bf16[8192,4096]{1,0:T(8,128)(2,1)} %p_ref.11), custom_call_target="tpu_custom_call" | custom-call | flops 1024 | bytes 1024 | tf_op jit(solution)/shard_map/pallas_call | solution.py:65
  83.6 1.7 %collective-permute-start.8 = (bf16[512,1024]{1,0:T(8,128)(2,1)S(1)}, bf16[512,1024]{1,0:T(8,128)(2,1)S(1)}, u32[]{:S(2)}, u32[]{:S(2)}) collective-permute-start(bf16[512,1024]{1,0:T(8,128)(2,1)S(1)} %shard_map.86), channel_id=1, source_target_pairs={{0,4},{1,3},{2,6},{3,1},{4,0},{5,7},{6,2},{7,5},{8,12},{9,11},{10,... | collective-permute-start | bytes 3145736 | tf_op jit(solution)/shard_map/ppermute | solution.py:46
  85.3 1.6 %collective-permute-start.5 = (bf16[256,1024]{1,0:T(8,128)(2,1)S(1)}, bf16[256,1024]{1,0:T(8,128)(2,1)S(1)}, u32[]{:S(2)}, u32[]{:S(2)}) collective-permute-start(bf16[256,1024]{1,0:T(8,128)(2,1)S(1)} %pad_maximum_fusion.4), channel_id=1, source_target_pairs={{0,2},{1,9},{2,0},{3,11},{4,6},{5,13},{6,4},{7,15},{8,10},{9,1},{1... | collective-permute-start | bytes 1572872 | tf_op jit(solution)/shard_map/ppermute | solution.py:46
  86.9 12.5 %shard_map.87 = f32[512,1024]{1,0:T(8,128)S(1)} custom-call(s32[4]{0:T(128)S(1)} %get-tuple-element.59.blocks_ref, bf16[512,8192]{1,0:T(8,128)(2,1)S(1)} %bitcast.24, bf16[8192,4096]{1,0:T(8,128)(2,1)} %p_ref.11), custom_call_target="tpu_custom_call" | custom-call | flops 1024 | bytes 1024 | tf_op jit(solution)/shard_map/pallas_call | solution.py:65
  99.4 0.2 slice_add_fusion.1
  99.7 0.5 collective-permute-start.7
  100.2 3.2 %collective-permute-done.8 = bf16[512,1024]{1,0:T(8,128)(2,1)S(1)} collective-permute-done((bf16[512,1024]{1,0:T(8,128)(2,1)S(1)}, bf16[512,1024]{1,0:T(8,128)(2,1)S(1)}, u32[]{:S(2)}, u32[]{:S(2)}) %collective-permute-start.8) | collective-permute-done | bytes 1048608 | tf_op jit(solution)/shard_map/ppermute | solution.py:46
  103.4 0.4 convert_add_fusion
  104.0 3.1 %collective-permute-start.9 = (bf16[512,512]{1,0:T(8,128)(2,1)S(1)}, bf16[512,512]{1,0:T(8,128)(2,1)S(1)}, u32[]{:S(2)}, u32[]{:S(2)}) collective-permute-start(bf16[512,512]{1,0:T(8,128)(2,1)S(1)} %slice.169), channel_id=1, source_target_pairs={{0,2},{1,9},{2,0},{3,11},{4,6},{5,13},{6,4},{7,15},{8,10},{9,1},{1... | collective-permute-start | bytes 1572872 | tf_op jit(solution)/shard_map/ppermute | solution.py:46
  107.2 11.9 %collective-permute-done.9 = bf16[512,512]{1,0:T(8,128)(2,1)S(1)} collective-permute-done((bf16[512,512]{1,0:T(8,128)(2,1)S(1)}, bf16[512,512]{1,0:T(8,128)(2,1)S(1)}, u32[]{:S(2)}, u32[]{:S(2)}) %collective-permute-start.9) | collective-permute-done | bytes 524320 | tf_op jit(solution)/shard_map/ppermute | solution.py:46
  119.0 0.2 slice_add_fusion
  119.2 0.7 slice.171
  119.9 2.3 %collective-permute-done.7 = bf16[256,2048]{1,0:T(8,128)(2,1)S(1)} collective-permute-done((bf16[256,2048]{1,0:T(8,128)(2,1)S(1)}, bf16[256,2048]{1,0:T(8,128)(2,1)S(1)}, u32[]{:S(2)}, u32[]{:S(2)}) %collective-permute-start.7) | collective-permute-done | bytes 1048608 | tf_op jit(solution)/shard_map/ppermute | solution.py:46
  122.2 0.2 pad_maximum_fusion.target_ref
  122.5 1.8 %shard_map.88.own_ref = bf16[256,512]{1,0:T(8,128)(2,1)S(1)} custom-call(s32[8]{0:T(128)S(1)} %bitcast.25, bf16[256,4096]{1,0:T(8,128)(2,1)S(1)} %pad_maximum_fusion.target_ref, bf16[4096,512]{1,0:T(8,128)(2,1)S(1)} %copy-done.2), custom_call_target="tpu_custom_call" | custom-call | flops 1024 | bytes 1024 | tf_op jit(solution)/shard_map/pallas_call | solution.py:101
  124.2 3.9 %collective-permute-start.10 = (bf16[256,512]{1,0:T(8,128)(2,1)S(1)}, bf16[256,512]{1,0:T(8,128)(2,1)S(1)}, u32[]{:S(2)}, u32[]{:S(2)}) collective-permute-start(bf16[256,512]{1,0:T(8,128)(2,1)S(1)} %shard_map.88.own_ref), channel_id=1, source_target_pairs={{0,1},{1,0},{2,3},{3,2},{4,5},{5,4},{6,7},{7,6},{8,9},{9,8},{10,11... | collective-permute-start | bytes 786440 | tf_op jit(solution)/shard_map/ppermute | solution.py:248
  128.3 6.3 %collective-permute-done.11.refs_1_ = bf16[512,256]{1,0:T(8,128)(2,1)S(1)} collective-permute-done((bf16[512,256]{1,0:T(8,128)(2,1)}, bf16[512,256]{1,0:T(8,128)(2,1)S(1)}, u32[]{:S(2)}, u32[]{:S(2)}) %collective-permute-start.11) | collective-permute-done | bytes 262176 | tf_op jit(solution)/shard_map/ppermute | solution.py:46
  134.6 1.3 shard_map.89
  136.1 1.3 collective-permute-start.14
  137.4 3.0 %collective-permute-start.15 = (bf16[64,512]{1,0:T(8,128)(2,1)S(1)}, bf16[64,512]{1,0:T(8,128)(2,1)S(1)}, u32[]{:S(2)}, u32[]{:S(2)}) collective-permute-start(bf16[64,512]{1,0:T(8,128)(2,1)S(1)} %get-tuple-element.74), channel_id=1, source_target_pairs={{0,12},{2,14},{4,8},{6,10},{8,4},{10,6},{12,0},{14,2},{1,11},{3,9}... | collective-permute-start | bytes 196616 | tf_op jit(solution)/shard_map/ppermute | solution.py:279
  140.4 0.6 collective-permute-start.16
  141.1 1.5 collective-permute-done.13
  142.6 1.6 %collective-permute-start.18 = (bf16[64,512]{1,0:T(8,128)(2,1)S(1)}, bf16[64,512]{1,0:T(8,128)(2,1)S(1)}, u32[]{:S(2)}, u32[]{:S(2)}) collective-permute-start(bf16[64,512]{1,0:T(8,128)(2,1)S(1)} %get-tuple-element.77), channel_id=1, source_target_pairs={{0,6},{2,4},{4,2},{6,0},{8,14},{10,12},{12,10},{14,8},{1,7},{3,5},... | collective-permute-start | bytes 196616 | tf_op jit(solution)/shard_map/ppermute | solution.py:279
  144.1 3.1 %collective-permute-start.19 = (bf16[64,512]{1,0:T(8,128)(2,1)S(1)}, bf16[64,512]{1,0:T(8,128)(2,1)S(1)}, u32[]{:S(2)}, u32[]{:S(2)}) collective-permute-start(bf16[64,512]{1,0:T(8,128)(2,1)S(1)} %get-tuple-element.78), channel_id=1, source_target_pairs={{0,14},{2,12},{4,10},{6,8},{8,6},{10,4},{12,2},{14,0},{1,15},{3,13... | collective-permute-start | bytes 196616 | tf_op jit(solution)/shard_map/ppermute | solution.py:279
  147.2 1.4 collective-permute-done.17
  148.6 0.3 collective-permute-done.18
  148.9 2.2 %collective-permute-done.19 = bf16[64,512]{1,0:T(8,128)(2,1)S(1)} collective-permute-done((bf16[64,512]{1,0:T(8,128)(2,1)S(1)}, bf16[64,512]{1,0:T(8,128)(2,1)S(1)}, u32[]{:S(2)}, u32[]{:S(2)}) %collective-permute-start.19) | collective-permute-done | bytes 65568 | tf_op jit(solution)/shard_map/ppermute | solution.py:279
  151.1 0.7 add_bitcast_fusion
  (56 shorter events, 1.3 us)
Async XLA Ops:
  0.8 2.2 %copy-start = (bf16[256,8192]{1,0:T(8,128)(2,1)S(1)}, bf16[256,8192]{1,0:T(8,128)(2,1)}, u32[]{:S(2)}) copy-start(bf16[256,8192]{1,0:T(8,128)(2,1)} %g_ref.7) | copy-start | bytes 12582916
  17.8 3.6 %copy-start.1 = (bf16[256,8192]{1,0:T(8,128)(2,1)S(1)}, bf16[256,8192]{1,0:T(8,128)(2,1)}, u32[]{:S(2)}) copy-start(bf16[256,8192]{1,0:T(8,128)(2,1)} %g_ref.7) | copy-start | bytes 12582916
  18.0 21.3 %slice-start = ((s8[8388608]{0:T(1024)(128)(4,1)}), s8[4194304]{0:T(1024)(128)(4,1)S(1)}, s32[]{:S(2)}) async-start(s8[8388608]{0:T(1024)(128)(4,1)} %bitcast.23), calls=%async_computation | async-start | bytes 8388608
  18.3 18.3 %collective-permute-start = (f16[272,2048]{1,0:T(8,128)(2,1)S(1)}, f16[272,2048]{1,0:T(8,128)(2,1)S(1)}, u32[]{:S(2)}, u32[]{:S(2)}) collective-permute-start(f16[272,2048]{1,0:T(8,128)(2,1)S(1)} %pad_maximum_fusion.1), channel_id=1, source_target_pairs={{0,4},{1,3},{2,6},{3,1},{4,0},{5,7},{6,2},{7,5},{8,12},{9,11},{10,... | collective-permute-start | bytes 3342344 | tf_op jit(solution)/shard_map/ppermute | solution.py:46
  21.4 17.9 %slice-start.1 = ((s8[8388608]{0:T(1024)(128)(4,1)}), s8[4194304]{0:T(1024)(128)(4,1)S(1)}, s32[]{:S(2)}) async-start(s8[8388608]{0:T(1024)(128)(4,1)} %bitcast.23), calls=%async_computation.1 | async-start | bytes 8388608
  37.5 14.1 %collective-permute-start.1 = (f16[272,1024]{1,0:T(8,128)(2,1)S(1)}, f16[272,1024]{1,0:T(8,128)(2,1)S(1)}, u32[]{:S(2)}, u32[]{:S(2)}) collective-permute-start(f16[272,1024]{1,0:T(8,128)(2,1)S(1)} %pad_maximum_fusion.3), channel_id=1, source_target_pairs={{0,2},{1,9},{2,0},{3,11},{4,6},{5,13},{6,4},{7,15},{8,10},{9,1},{1... | collective-permute-start | bytes 1671176 | tf_op jit(solution)/shard_map/ppermute | solution.py:46
  52.0 15.8 %collective-permute-start.4 = (bf16[512,1024]{1,0:T(8,128)(2,1)S(1)}, bf16[512,1024]{1,0:T(8,128)(2,1)S(1)}, u32[]{:S(2)}, u32[]{:S(2)}) collective-permute-start(bf16[512,1024]{1,0:T(8,128)(2,1)S(1)} %shard_map.84), channel_id=1, source_target_pairs={{0,2},{1,5},{2,0},{3,7},{4,6},{5,1},{6,4},{7,3},{8,10},{9,13},{10,... | collective-permute-start | bytes 3145736 | tf_op jit(solution)/shard_map/ppermute | solution.py:46
  52.4 15.1 %collective-permute-start.2 = (f16[272,512]{1,0:T(8,128)(2,1)S(1)}, f16[272,512]{1,0:T(8,128)(2,1)S(1)}, u32[]{:S(2)}, u32[]{:S(2)}) collective-permute-start(f16[272,512]{1,0:T(8,128)(2,1)S(1)} %pad_maximum_fusion.5), channel_id=1, source_target_pairs={{0,8},{1,5},{2,10},{3,7},{4,12},{5,1},{6,14},{7,3},{8,0},{9,13},{1... | collective-permute-start | bytes 835592 | tf_op jit(solution)/shard_map/ppermute | solution.py:46
  67.7 17.6 %collective-permute-start.3 = (bf16[256,512]{1,0:T(8,128)(2,1)S(1)}, bf16[256,512]{1,0:T(8,128)(2,1)S(1)}, u32[]{:S(2)}, u32[]{:S(2)}) collective-permute-start(bf16[256,512]{1,0:T(8,128)(2,1)S(1)} %fusion), channel_id=1, source_target_pairs={{0,8},{1,5},{2,10},{3,7},{4,12},{5,1},{6,14},{7,3},{8,0},{9,13},{1... | collective-permute-start | bytes 786440 | tf_op jit(solution)/shard_map/ppermute | solution.py:46
  68.4 31.0 %collective-permute-start.6 = (bf16[512,512]{1,0:T(8,128)(2,1)S(1)}, bf16[512,512]{1,0:T(8,128)(2,1)S(1)}, u32[]{:S(2)}, u32[]{:S(2)}) collective-permute-start(bf16[512,512]{1,0:T(8,128)(2,1)S(1)} %slice.166), channel_id=1, source_target_pairs={{0,8},{1,3},{2,10},{3,1},{4,12},{5,7},{6,14},{7,5},{8,0},{9,11},{1... | collective-permute-start | bytes 1572872 | tf_op jit(solution)/shard_map/ppermute | solution.py:46
  83.6 19.8 %collective-permute-start.8 = (bf16[512,1024]{1,0:T(8,128)(2,1)S(1)}, bf16[512,1024]{1,0:T(8,128)(2,1)S(1)}, u32[]{:S(2)}, u32[]{:S(2)}) collective-permute-start(bf16[512,1024]{1,0:T(8,128)(2,1)S(1)} %shard_map.86), channel_id=1, source_target_pairs={{0,4},{1,3},{2,6},{3,1},{4,0},{5,7},{6,2},{7,5},{8,12},{9,11},{10,... | collective-permute-start | bytes 3145736 | tf_op jit(solution)/shard_map/ppermute | solution.py:46
  85.3 14.3 %collective-permute-start.5 = (bf16[256,1024]{1,0:T(8,128)(2,1)S(1)}, bf16[256,1024]{1,0:T(8,128)(2,1)S(1)}, u32[]{:S(2)}, u32[]{:S(2)}) collective-permute-start(bf16[256,1024]{1,0:T(8,128)(2,1)S(1)} %pad_maximum_fusion.4), channel_id=1, source_target_pairs={{0,2},{1,9},{2,0},{3,11},{4,6},{5,13},{6,4},{7,15},{8,10},{9,1},{1... | collective-permute-start | bytes 1572872 | tf_op jit(solution)/shard_map/ppermute | solution.py:46
  99.7 22.5 %collective-permute-start.7 = (bf16[256,2048]{1,0:T(8,128)(2,1)S(1)}, bf16[256,2048]{1,0:T(8,128)(2,1)S(1)}, u32[]{:S(2)}, u32[]{:S(2)}) collective-permute-start(bf16[256,2048]{1,0:T(8,128)(2,1)S(1)} %pad_maximum_fusion.2), channel_id=1, source_target_pairs={{0,4},{1,3},{2,6},{3,1},{4,0},{5,7},{6,2},{7,5},{8,12},{9,11},{10,... | collective-permute-start | bytes 3145736 | tf_op jit(solution)/shard_map/ppermute | solution.py:46
  104.0 15.0 %collective-permute-start.9 = (bf16[512,512]{1,0:T(8,128)(2,1)S(1)}, bf16[512,512]{1,0:T(8,128)(2,1)S(1)}, u32[]{:S(2)}, u32[]{:S(2)}) collective-permute-start(bf16[512,512]{1,0:T(8,128)(2,1)S(1)} %slice.169), channel_id=1, source_target_pairs={{0,2},{1,9},{2,0},{3,11},{4,6},{5,13},{6,4},{7,15},{8,10},{9,1},{1... | collective-permute-start | bytes 1572872 | tf_op jit(solution)/shard_map/ppermute | solution.py:46
  107.1 21.2 %collective-permute-start.12 = (bf16[512,256]{1,0:T(8,128)(2,1)S(1)}, bf16[512,256]{1,0:T(8,128)(2,1)S(1)}, u32[]{:S(2)}, u32[]{:S(2)}) collective-permute-start(bf16[512,256]{1,0:T(8,128)(2,1)S(1)} %slice.170), channel_id=1, source_target_pairs={{0,4},{1,9},{2,6},{3,11},{4,0},{5,13},{6,2},{7,15},{8,12},{9,1},{1... | collective-permute-start | bytes 786440 | tf_op jit(solution)/shard_map/ppermute | solution.py:46
  119.9 2.5 %copy-start.2 = (bf16[4096,512]{1,0:T(8,128)(2,1)S(1)}, bf16[4096,512]{1,0:T(8,128)(2,1)}, u32[]{:S(2)}) copy-start(bf16[4096,512]{1,0:T(8,128)(2,1)} %inverse_ref.1) | copy-start | bytes 12582916
  119.9 14.7 %collective-permute-start.11 = (bf16[512,256]{1,0:T(8,128)(2,1)}, bf16[512,256]{1,0:T(8,128)(2,1)S(1)}, u32[]{:S(2)}, u32[]{:S(2)}) collective-permute-start(bf16[512,256]{1,0:T(8,128)(2,1)} %slice.171), channel_id=1, source_target_pairs={{0,8},{1,5},{2,10},{3,7},{4,12},{5,1},{6,14},{7,3},{8,0},{9,13},{1... | collective-permute-start | bytes 786440 | tf_op jit(solution)/shard_map/ppermute | solution.py:46
  122.4 5.7 %copy-start.3 = (s32[2,8]{1,0:T(2,128)S(1)}, s32[2,8]{1,0:T(2,128)}, u32[]{:S(2)}) copy-start(s32[2,8]{1,0:T(2,128)} %constant.47.clone) | copy-start | bytes 196
  124.2 10.4 %collective-permute-start.10 = (bf16[256,512]{1,0:T(8,128)(2,1)S(1)}, bf16[256,512]{1,0:T(8,128)(2,1)S(1)}, u32[]{:S(2)}, u32[]{:S(2)}) collective-permute-start(bf16[256,512]{1,0:T(8,128)(2,1)S(1)} %shard_map.88.own_ref), channel_id=1, source_target_pairs={{0,1},{1,0},{2,3},{3,2},{4,5},{5,4},{6,7},{7,6},{8,9},{9,8},{10,11... | collective-permute-start | bytes 786440 | tf_op jit(solution)/shard_map/ppermute | solution.py:248
  136.0 6.6 %collective-permute-start.13 = (bf16[64,512]{1,0:T(8,128)(2,1)S(1)}, bf16[64,512]{1,0:T(8,128)(2,1)S(1)}, u32[]{:S(2)}, u32[]{:S(2)}) collective-permute-start(bf16[64,512]{1,0:T(8,128)(2,1)S(1)} %get-tuple-element.72), channel_id=1, source_target_pairs={{0,8},{2,10},{4,12},{6,14},{8,0},{10,2},{12,4},{14,6},{1,9},{3,11}... | collective-permute-start | bytes 196616 | tf_op jit(solution)/shard_map/ppermute | solution.py:279
  136.1 8.1 %collective-permute-start.14 = (bf16[64,512]{1,0:T(8,128)(2,1)S(1)}, bf16[64,512]{1,0:T(8,128)(2,1)S(1)}, u32[]{:S(2)}, u32[]{:S(2)}) collective-permute-start(bf16[64,512]{1,0:T(8,128)(2,1)S(1)} %get-tuple-element.73), channel_id=1, source_target_pairs={{0,4},{2,6},{4,0},{6,2},{8,12},{10,14},{12,8},{14,10},{1,3},{3,1},... | collective-permute-start | bytes 196616 | tf_op jit(solution)/shard_map/ppermute | solution.py:279
  137.4 9.8 %collective-permute-start.15 = (bf16[64,512]{1,0:T(8,128)(2,1)S(1)}, bf16[64,512]{1,0:T(8,128)(2,1)S(1)}, u32[]{:S(2)}, u32[]{:S(2)}) collective-permute-start(bf16[64,512]{1,0:T(8,128)(2,1)S(1)} %get-tuple-element.74), channel_id=1, source_target_pairs={{0,12},{2,14},{4,8},{6,10},{8,4},{10,6},{12,0},{14,2},{1,11},{3,9}... | collective-permute-start | bytes 196616 | tf_op jit(solution)/shard_map/ppermute | solution.py:279
  140.4 6.8 %collective-permute-start.16 = (bf16[64,512]{1,0:T(8,128)(2,1)S(1)}, bf16[64,512]{1,0:T(8,128)(2,1)S(1)}, u32[]{:S(2)}, u32[]{:S(2)}) collective-permute-start(bf16[64,512]{1,0:T(8,128)(2,1)S(1)} %get-tuple-element.75), channel_id=1, source_target_pairs={{0,2},{2,0},{4,6},{6,4},{8,10},{10,8},{12,14},{14,12},{1,5},{3,7},... | collective-permute-start | bytes 196616 | tf_op jit(solution)/shard_map/ppermute | solution.py:279
  141.1 7.5 %collective-permute-start.17 = (bf16[64,512]{1,0:T(8,128)(2,1)S(1)}, bf16[64,512]{1,0:T(8,128)(2,1)S(1)}, u32[]{:S(2)}, u32[]{:S(2)}) collective-permute-start(bf16[64,512]{1,0:T(8,128)(2,1)S(1)} %get-tuple-element.76), channel_id=1, source_target_pairs={{0,10},{2,8},{4,14},{6,12},{8,2},{10,0},{12,6},{14,4},{1,13},{3,15... | collective-permute-start | bytes 196616 | tf_op jit(solution)/shard_map/ppermute | solution.py:279
  142.6 6.3 %collective-permute-start.18 = (bf16[64,512]{1,0:T(8,128)(2,1)S(1)}, bf16[64,512]{1,0:T(8,128)(2,1)S(1)}, u32[]{:S(2)}, u32[]{:S(2)}) collective-permute-start(bf16[64,512]{1,0:T(8,128)(2,1)S(1)} %get-tuple-element.77), channel_id=1, source_target_pairs={{0,6},{2,4},{4,2},{6,0},{8,14},{10,12},{12,10},{14,8},{1,7},{3,5},... | collective-permute-start | bytes 196616 | tf_op jit(solution)/shard_map/ppermute | solution.py:279
  144.1 7.0 %collective-permute-start.19 = (bf16[64,512]{1,0:T(8,128)(2,1)S(1)}, bf16[64,512]{1,0:T(8,128)(2,1)S(1)}, u32[]{:S(2)}, u32[]{:S(2)}) collective-permute-start(bf16[64,512]{1,0:T(8,128)(2,1)S(1)} %get-tuple-element.78), channel_id=1, source_target_pairs={{0,14},{2,12},{4,10},{6,8},{8,6},{10,4},{12,2},{14,0},{1,15},{3,13... | collective-permute-start | bytes 196616 | tf_op jit(solution)/shard_map/ppermute | solution.py:279

commit v4 on v3

--- a/solution.py
+++ b/solution.py
@@ -175,7 +175,7 @@
 
 
 STEPS = (
-    "TS", "sT0", "TK", "dT0", "sT1", "Sb", "dT1", "sT2", "sB0", "Kb", "dT2", "sG0", "dB0", "sB1", "Sa", "sA0", "dG0", "sG1", "Ka", "dB1", "dG1", "sG2", "dA0", "sA1", "sB2", "dA1", "sA2", "dG2", "F", "sE0", "dE0", "dB2", "dA2", "SC",
+    "TS", "sT0", "TK", "dT0", "sT1", "Sb", "dT1", "sT2", "sB0", "Kb", "dT2", "sG0", "dB0", "sB1", "Sa", "dG0", "sA0", "sG1", "Ka", "dB1", "dG1", "sG2", "dA0", "sA1", "sB2", "dA1", "sA2", "dG2", "F", "sE0", "dE0", "dB2", "dA2", "SC",
 )
 AXES = {"T": ("lxh", "xhl"), "L": ("xlh", "lxh"), "A": ("lxh", "xhl"), "B": ("xhl", "lxh")}
 

time: 152 us -> 152 us (level)
  no operation moved by 1% of the time
where the time goes in v4:
time: 152 us
  Pallas kernels  82.4 us (54%)
  starting transfers between devices  30.5 us (20%)
  waiting for transfers between devices  29.3 us (19%)
  other arithmetic  4.71 us (3%)
  local copies, waits for them, and re-layouts  4.49 us (3%)
    pallas_call x6, Pallas kernels, product(): pl.pallas_call(functools.partial(product_kernel, with_top), grid_spec=plt...  79.2 us
    ppermute x12, waiting for transfers between devices, swap(): return lax.ppermute(value, BOTH, self.perms[hop])  23.7 us
    ppermute x12, starting transfers between devices, swap(): return lax.ppermute(value, BOTH, self.perms[hop])  17.9 us
    ppermute x7, starting transfers between devices, on_device(): value = value + lax.ppermute(parts[i], BOTH, pairs).astype(F32)  9.66 us
    ppermute x7, waiting for transfers between devices, on_device(): value = value + lax.ppermute(parts[i], BOTH, pairs).astype(F32)  5.53 us
    unnamed x12, local copies, waits for them, and re-layouts  3.11 us
  transfers between devices with their start and end apart: 20, of which 8 were waited for; matrix products, arithmetic and copies ran while one was open for 2% of the time, Pallas kernels for 44%

profile of v4, /device:TPU:0, one launch (start us, length us, event | category | flops | bytes accessed | tf_op | source)
XLA Modules:
  0.0 151.7 jit_solution(7830121038945770809)
XLA Ops:
  0.0 0.7 broadcast_multiply_fusion
  0.8 2.2 %copy-done = bf16[256,8192]{1,0:T(8,128)(2,1)S(1)} copy-done((bf16[256,8192]{1,0:T(8,128)(2,1)S(1)}, bf16[256,8192]{1,0:T(8,128)(2,1)}, u32[]{:S(2)}) %copy-start) | copy-done | bytes 4194328
  3.0 14.7 %shard_map.82 = (f32[256,2048]{1,0:T(8,128)S(1)}, f32[8,2048]{1,0:T(8,128)S(1)}) custom-call(s32[4]{0:T(128)S(1)} %get-tuple-element.97.blocks_ref, bf16[256,8192]{1,0:T(8,128)(2,1)S(1)} %copy-done, bf16[8192,4096]{1,0:T(8,128)(2,1)} %p_ref.11), custom_call_target="tpu_custom_call" | custom-call | flops 1024 | bytes 1024 | tf_op jit(solution)/shard_map/pallas_call | solution.py:65
  17.8 0.2 multiply_convert_fusion
  18.0 0.3 pad_maximum_fusion.1
  18.3 3.1 %collective-permute-start = (f16[272,2048]{1,0:T(8,128)(2,1)S(1)}, f16[272,2048]{1,0:T(8,128)(2,1)S(1)}, u32[]{:S(2)}, u32[]{:S(2)}) collective-permute-start(f16[272,2048]{1,0:T(8,128)(2,1)S(1)} %pad_maximum_fusion.1), channel_id=1, source_target_pairs={{0,4},{1,3},{2,6},{3,1},{4,0},{5,7},{6,2},{7,5},{8,12},{9,11},{10,... | collective-permute-start | bytes 3342344 | tf_op jit(solution)/shard_map/ppermute | solution.py:46
  21.4 15.2 %shard_map.83 = (f32[256,2048]{1,0:T(8,128)S(1)}, f32[8,2048]{1,0:T(8,128)S(1)}) custom-call(s32[4]{0:T(128)S(1)} %get-tuple-element.46.blocks_ref, bf16[256,8192]{1,0:T(8,128)(2,1)S(1)} %copy-done.1, bf16[8192,4096]{1,0:T(8,128)(2,1)} %p_ref.11), custom_call_target="tpu_custom_call" | custom-call | flops 1024 | bytes 1024 | tf_op jit(solution)/shard_map/pallas_call | solution.py:65
  36.7 0.4 multiply_add_fusion
  37.2 0.1 multiply_convert_fusion.1
  37.3 0.1 pad_maximum_fusion.3
  37.5 1.8 %collective-permute-start.1 = (f16[272,1024]{1,0:T(8,128)(2,1)S(1)}, f16[272,1024]{1,0:T(8,128)(2,1)S(1)}, u32[]{:S(2)}, u32[]{:S(2)}) collective-permute-start(f16[272,1024]{1,0:T(8,128)(2,1)S(1)} %pad_maximum_fusion.3), channel_id=1, source_target_pairs={{0,2},{1,9},{2,0},{3,11},{4,6},{5,13},{6,4},{7,15},{8,10},{9,1},{1... | collective-permute-start | bytes 1671176 | tf_op jit(solution)/shard_map/ppermute | solution.py:46
  39.3 12.3 %shard_map.84 = bf16[512,1024]{1,0:T(8,128)(2,1)S(1)} custom-call(s32[4]{0:T(128)S(1)} %get-tuple-element.51.blocks_ref, bf16[512,8192]{1,0:T(8,128)(2,1)S(1)} %bitcast.24, bf16[8192,4096]{1,0:T(8,128)(2,1)} %p_ref.11), custom_call_target="tpu_custom_call" | custom-call | flops 1024 | bytes 1024 | tf_op jit(solution)/shard_map/pallas_call | solution.py:65
  51.6 0.2 slice_add_fusion.2
  52.0 0.4 collective-permute-start.4
  52.4 2.8 %collective-permute-start.2 = (f16[272,512]{1,0:T(8,128)(2,1)S(1)}, f16[272,512]{1,0:T(8,128)(2,1)S(1)}, u32[]{:S(2)}, u32[]{:S(2)}) collective-permute-start(f16[272,512]{1,0:T(8,128)(2,1)S(1)} %pad_maximum_fusion.5), channel_id=1, source_target_pairs={{0,8},{1,5},{2,10},{3,7},{4,12},{5,1},{6,14},{7,3},{8,0},{9,13},{1... | collective-permute-start | bytes 835592 | tf_op jit(solution)/shard_map/ppermute | solution.py:46
  55.3 12.3 %shard_map.85 = f32[512,1024]{1,0:T(8,128)S(1)} custom-call(s32[4]{0:T(128)S(1)} %get-tuple-element.55.blocks_ref, bf16[512,8192]{1,0:T(8,128)(2,1)S(1)} %bitcast.24, bf16[8192,4096]{1,0:T(8,128)(2,1)} %p_ref.11), custom_call_target="tpu_custom_call" | custom-call | flops 1024 | bytes 1024 | tf_op jit(solution)/shard_map/pallas_call | solution.py:65
  67.7 0.2 collective-permute-start.3
  68.0 0.4 convert_add_fusion.1
  68.5 2.8 %collective-permute-start.6 = (bf16[512,512]{1,0:T(8,128)(2,1)S(1)}, bf16[512,512]{1,0:T(8,128)(2,1)S(1)}, u32[]{:S(2)}, u32[]{:S(2)}) collective-permute-start(bf16[512,512]{1,0:T(8,128)(2,1)S(1)} %slice.166), channel_id=1, source_target_pairs={{0,8},{1,3},{2,10},{3,1},{4,12},{5,7},{6,14},{7,5},{8,0},{9,11},{1... | collective-permute-start | bytes 1572872 | tf_op jit(solution)/shard_map/ppermute | solution.py:46
  71.3 12.3 %shard_map.86 = bf16[512,1024]{1,0:T(8,128)(2,1)S(1)} custom-call(s32[4]{0:T(128)S(1)} %get-tuple-element.59.blocks_ref, bf16[512,8192]{1,0:T(8,128)(2,1)S(1)} %bitcast.24, bf16[8192,4096]{1,0:T(8,128)(2,1)} %p_ref.11), custom_call_target="tpu_custom_call" | custom-call | flops 1024 | bytes 1024 | tf_op jit(solution)/shard_map/pallas_call | solution.py:65
  83.7 1.7 %collective-permute-start.8 = (bf16[512,1024]{1,0:T(8,128)(2,1)S(1)}, bf16[512,1024]{1,0:T(8,128)(2,1)S(1)}, u32[]{:S(2)}, u32[]{:S(2)}) collective-permute-start(bf16[512,1024]{1,0:T(8,128)(2,1)S(1)} %shard_map.86), channel_id=1, source_target_pairs={{0,4},{1,3},{2,6},{3,1},{4,0},{5,7},{6,2},{7,5},{8,12},{9,11},{10,... | collective-permute-start | bytes 3145736 | tf_op jit(solution)/shard_map/ppermute | solution.py:46
  85.4 1.5 collective-permute-start.5
  86.8 12.5 %shard_map.87 = f32[512,1024]{1,0:T(8,128)S(1)} custom-call(s32[4]{0:T(128)S(1)} %get-tuple-element.63.blocks_ref, bf16[512,8192]{1,0:T(8,128)(2,1)S(1)} %bitcast.24, bf16[8192,4096]{1,0:T(8,128)(2,1)} %p_ref.11), custom_call_target="tpu_custom_call" | custom-call | flops 1024 | bytes 1024 | tf_op jit(solution)/shard_map/pallas_call | solution.py:65
  99.4 0.2 slice_add_fusion.1
  99.6 0.5 collective-permute-start.7
  100.1 4.1 %collective-permute-done.8 = bf16[512,1024]{1,0:T(8,128)(2,1)S(1)} collective-permute-done((bf16[512,1024]{1,0:T(8,128)(2,1)S(1)}, bf16[512,1024]{1,0:T(8,128)(2,1)S(1)}, u32[]{:S(2)}, u32[]{:S(2)}) %collective-permute-start.8) | collective-permute-done | bytes 1048608 | tf_op jit(solution)/shard_map/ppermute | solution.py:46
  104.2 0.4 convert_add_fusion
  104.7 3.1 %collective-permute-start.9 = (bf16[512,512]{1,0:T(8,128)(2,1)S(1)}, bf16[512,512]{1,0:T(8,128)(2,1)S(1)}, u32[]{:S(2)}, u32[]{:S(2)}) collective-permute-start(bf16[512,512]{1,0:T(8,128)(2,1)S(1)} %slice.169), channel_id=1, source_target_pairs={{0,2},{1,9},{2,0},{3,11},{4,6},{5,13},{6,4},{7,15},{8,10},{9,1},{1... | collective-permute-start | bytes 1572872 | tf_op jit(solution)/shard_map/ppermute | solution.py:46
  107.9 12.7 %collective-permute-done.9 = bf16[512,512]{1,0:T(8,128)(2,1)S(1)} collective-permute-done((bf16[512,512]{1,0:T(8,128)(2,1)S(1)}, bf16[512,512]{1,0:T(8,128)(2,1)S(1)}, u32[]{:S(2)}, u32[]{:S(2)}) %collective-permute-start.9) | collective-permute-done | bytes 524320 | tf_op jit(solution)/shard_map/ppermute | solution.py:46
  120.6 0.2 slice_add_fusion
  120.8 0.7 slice.171
  121.5 1.1 collective-permute-done.7
  122.6 0.2 pad_maximum_fusion.target_ref
  122.8 0.9 copy-done.2
  123.7 1.8 %shard_map.88.own_ref = bf16[256,512]{1,0:T(8,128)(2,1)S(1)} custom-call(s32[8]{0:T(128)S(1)} %bitcast.25, bf16[256,4096]{1,0:T(8,128)(2,1)S(1)} %pad_maximum_fusion.target_ref, bf16[4096,512]{1,0:T(8,128)(2,1)S(1)} %copy-done.2), custom_call_target="tpu_custom_call" | custom-call | flops 1024 | bytes 1024 | tf_op jit(solution)/shard_map/pallas_call | solution.py:101
  125.5 2.9 %collective-permute-start.10 = (bf16[256,512]{1,0:T(8,128)(2,1)S(1)}, bf16[256,512]{1,0:T(8,128)(2,1)S(1)}, u32[]{:S(2)}, u32[]{:S(2)}) collective-permute-start(bf16[256,512]{1,0:T(8,128)(2,1)S(1)} %shard_map.88.own_ref), channel_id=1, source_target_pairs={{0,1},{1,0},{2,3},{3,2},{4,5},{5,4},{6,7},{7,6},{8,9},{9,8},{10,11... | collective-permute-start | bytes 786440 | tf_op jit(solution)/shard_map/ppermute | solution.py:248
  128.5 5.9 %collective-permute-done.11.refs_1_ = bf16[512,256]{1,0:T(8,128)(2,1)S(1)} collective-permute-done((bf16[512,256]{1,0:T(8,128)(2,1)}, bf16[512,256]{1,0:T(8,128)(2,1)S(1)}, u32[]{:S(2)}, u32[]{:S(2)}) %collective-permute-start.11) | collective-permute-done | bytes 262176 | tf_op jit(solution)/shard_map/ppermute | solution.py:46
  134.4 1.3 shard_map.89
  135.8 1.6 %collective-permute-start.14 = (bf16[64,512]{1,0:T(8,128)(2,1)S(1)}, bf16[64,512]{1,0:T(8,128)(2,1)S(1)}, u32[]{:S(2)}, u32[]{:S(2)}) collective-permute-start(bf16[64,512]{1,0:T(8,128)(2,1)S(1)} %get-tuple-element.77), channel_id=1, source_target_pairs={{0,4},{2,6},{4,0},{6,2},{8,12},{10,14},{12,8},{14,10},{1,3},{3,1},... | collective-permute-start | bytes 196616 | tf_op jit(solution)/shard_map/ppermute | solution.py:279
  137.5 2.8 %collective-permute-start.15 = (bf16[64,512]{1,0:T(8,128)(2,1)S(1)}, bf16[64,512]{1,0:T(8,128)(2,1)S(1)}, u32[]{:S(2)}, u32[]{:S(2)}) collective-permute-start(bf16[64,512]{1,0:T(8,128)(2,1)S(1)} %get-tuple-element.78), channel_id=1, source_target_pairs={{0,12},{2,14},{4,8},{6,10},{8,4},{10,6},{12,0},{14,2},{1,11},{3,9}... | collective-permute-start | bytes 196616 | tf_op jit(solution)/shard_map/ppermute | solution.py:279
  140.2 0.7 collective-permute-start.16
  140.9 1.5 %collective-permute-done.13 = bf16[64,512]{1,0:T(8,128)(2,1)S(1)} collective-permute-done((bf16[64,512]{1,0:T(8,128)(2,1)S(1)}, bf16[64,512]{1,0:T(8,128)(2,1)S(1)}, u32[]{:S(2)}, u32[]{:S(2)}) %collective-permute-start.13) | collective-permute-done | bytes 65568 | tf_op jit(solution)/shard_map/ppermute | solution.py:279
  142.4 1.6 %collective-permute-start.18 = (bf16[64,512]{1,0:T(8,128)(2,1)S(1)}, bf16[64,512]{1,0:T(8,128)(2,1)S(1)}, u32[]{:S(2)}, u32[]{:S(2)}) collective-permute-start(bf16[64,512]{1,0:T(8,128)(2,1)S(1)} %get-tuple-element.81), channel_id=1, source_target_pairs={{0,6},{2,4},{4,2},{6,0},{8,14},{10,12},{12,10},{14,8},{1,7},{3,5},... | collective-permute-start | bytes 196616 | tf_op jit(solution)/shard_map/ppermute | solution.py:279
  144.0 3.0 %collective-permute-start.19 = (bf16[64,512]{1,0:T(8,128)(2,1)S(1)}, bf16[64,512]{1,0:T(8,128)(2,1)S(1)}, u32[]{:S(2)}, u32[]{:S(2)}) collective-permute-start(bf16[64,512]{1,0:T(8,128)(2,1)S(1)} %get-tuple-element.82), channel_id=1, source_target_pairs={{0,14},{2,12},{4,10},{6,8},{8,6},{10,4},{12,2},{14,0},{1,15},{3,13... | collective-permute-start | bytes 196616 | tf_op jit(solution)/shard_map/ppermute | solution.py:279
  147.0 1.5 collective-permute-done.17
  148.5 0.2 collective-permute-done.18
  148.7 2.3 %collective-permute-done.19 = bf16[64,512]{1,0:T(8,128)(2,1)S(1)} collective-permute-done((bf16[64,512]{1,0:T(8,128)(2,1)S(1)}, bf16[64,512]{1,0:T(8,128)(2,1)S(1)}, u32[]{:S(2)}, u32[]{:S(2)}) %collective-permute-start.19) | collective-permute-done | bytes 65568 | tf_op jit(solution)/shard_map/ppermute | solution.py:279
  151.0 0.7 add_bitcast_fusion
  (56 shorter events, 1.4 us)
Async XLA Ops:
  0.8 2.2 %copy-start = (bf16[256,8192]{1,0:T(8,128)(2,1)S(1)}, bf16[256,8192]{1,0:T(8,128)(2,1)}, u32[]{:S(2)}) copy-start(bf16[256,8192]{1,0:T(8,128)(2,1)} %g_ref.7) | copy-start | bytes 12582916
  17.8 3.6 %copy-start.1 = (bf16[256,8192]{1,0:T(8,128)(2,1)S(1)}, bf16[256,8192]{1,0:T(8,128)(2,1)}, u32[]{:S(2)}) copy-start(bf16[256,8192]{1,0:T(8,128)(2,1)} %g_ref.7) | copy-start | bytes 12582916
  18.0 21.3 %slice-start = ((s8[8388608]{0:T(1024)(128)(4,1)}), s8[4194304]{0:T(1024)(128)(4,1)S(1)}, s32[]{:S(2)}) async-start(s8[8388608]{0:T(1024)(128)(4,1)} %bitcast.23), calls=%async_computation | async-start | bytes 8388608
  18.3 18.3 %collective-permute-start = (f16[272,2048]{1,0:T(8,128)(2,1)S(1)}, f16[272,2048]{1,0:T(8,128)(2,1)S(1)}, u32[]{:S(2)}, u32[]{:S(2)}) collective-permute-start(f16[272,2048]{1,0:T(8,128)(2,1)S(1)} %pad_maximum_fusion.1), channel_id=1, source_target_pairs={{0,4},{1,3},{2,6},{3,1},{4,0},{5,7},{6,2},{7,5},{8,12},{9,11},{10,... | collective-permute-start | bytes 3342344 | tf_op jit(solution)/shard_map/ppermute | solution.py:46
  21.4 17.9 %slice-start.1 = ((s8[8388608]{0:T(1024)(128)(4,1)}), s8[4194304]{0:T(1024)(128)(4,1)S(1)}, s32[]{:S(2)}) async-start(s8[8388608]{0:T(1024)(128)(4,1)} %bitcast.23), calls=%async_computation.1 | async-start | bytes 8388608
  37.5 14.1 %collective-permute-start.1 = (f16[272,1024]{1,0:T(8,128)(2,1)S(1)}, f16[272,1024]{1,0:T(8,128)(2,1)S(1)}, u32[]{:S(2)}, u32[]{:S(2)}) collective-permute-start(f16[272,1024]{1,0:T(8,128)(2,1)S(1)} %pad_maximum_fusion.3), channel_id=1, source_target_pairs={{0,2},{1,9},{2,0},{3,11},{4,6},{5,13},{6,4},{7,15},{8,10},{9,1},{1... | collective-permute-start | bytes 1671176 | tf_op jit(solution)/shard_map/ppermute | solution.py:46
  52.0 15.9 %collective-permute-start.4 = (bf16[512,1024]{1,0:T(8,128)(2,1)S(1)}, bf16[512,1024]{1,0:T(8,128)(2,1)S(1)}, u32[]{:S(2)}, u32[]{:S(2)}) collective-permute-start(bf16[512,1024]{1,0:T(8,128)(2,1)S(1)} %shard_map.84), channel_id=1, source_target_pairs={{0,2},{1,5},{2,0},{3,7},{4,6},{5,1},{6,4},{7,3},{8,10},{9,13},{10,... | collective-permute-start | bytes 3145736 | tf_op jit(solution)/shard_map/ppermute | solution.py:46
  52.4 15.2 %collective-permute-start.2 = (f16[272,512]{1,0:T(8,128)(2,1)S(1)}, f16[272,512]{1,0:T(8,128)(2,1)S(1)}, u32[]{:S(2)}, u32[]{:S(2)}) collective-permute-start(f16[272,512]{1,0:T(8,128)(2,1)S(1)} %pad_maximum_fusion.5), channel_id=1, source_target_pairs={{0,8},{1,5},{2,10},{3,7},{4,12},{5,1},{6,14},{7,3},{8,0},{9,13},{1... | collective-permute-start | bytes 835592 | tf_op jit(solution)/shard_map/ppermute | solution.py:46
  67.7 15.9 %collective-permute-start.3 = (bf16[256,512]{1,0:T(8,128)(2,1)S(1)}, bf16[256,512]{1,0:T(8,128)(2,1)S(1)}, u32[]{:S(2)}, u32[]{:S(2)}) collective-permute-start(bf16[256,512]{1,0:T(8,128)(2,1)S(1)} %fusion), channel_id=1, source_target_pairs={{0,8},{1,5},{2,10},{3,7},{4,12},{5,1},{6,14},{7,3},{8,0},{9,13},{1... | collective-permute-start | bytes 786440 | tf_op jit(solution)/shard_map/ppermute | solution.py:46
  68.5 30.9 %collective-permute-start.6 = (bf16[512,512]{1,0:T(8,128)(2,1)S(1)}, bf16[512,512]{1,0:T(8,128)(2,1)S(1)}, u32[]{:S(2)}, u32[]{:S(2)}) collective-permute-start(bf16[512,512]{1,0:T(8,128)(2,1)S(1)} %slice.166), channel_id=1, source_target_pairs={{0,8},{1,3},{2,10},{3,1},{4,12},{5,7},{6,14},{7,5},{8,0},{9,11},{1... | collective-permute-start | bytes 1572872 | tf_op jit(solution)/shard_map/ppermute | solution.py:46
  83.7 20.5 %collective-permute-start.8 = (bf16[512,1024]{1,0:T(8,128)(2,1)S(1)}, bf16[512,1024]{1,0:T(8,128)(2,1)S(1)}, u32[]{:S(2)}, u32[]{:S(2)}) collective-permute-start(bf16[512,1024]{1,0:T(8,128)(2,1)S(1)} %shard_map.86), channel_id=1, source_target_pairs={{0,4},{1,3},{2,6},{3,1},{4,0},{5,7},{6,2},{7,5},{8,12},{9,11},{10,... | collective-permute-start | bytes 3145736 | tf_op jit(solution)/shard_map/ppermute | solution.py:46
  85.4 14.2 %collective-permute-start.5 = (bf16[256,1024]{1,0:T(8,128)(2,1)S(1)}, bf16[256,1024]{1,0:T(8,128)(2,1)S(1)}, u32[]{:S(2)}, u32[]{:S(2)}) collective-permute-start(bf16[256,1024]{1,0:T(8,128)(2,1)S(1)} %pad_maximum_fusion.4), channel_id=1, source_target_pairs={{0,2},{1,9},{2,0},{3,11},{4,6},{5,13},{6,4},{7,15},{8,10},{9,1},{1... | collective-permute-start | bytes 1572872 | tf_op jit(solution)/shard_map/ppermute | solution.py:46
  99.6 22.9 %collective-permute-start.7 = (bf16[256,2048]{1,0:T(8,128)(2,1)S(1)}, bf16[256,2048]{1,0:T(8,128)(2,1)S(1)}, u32[]{:S(2)}, u32[]{:S(2)}) collective-permute-start(bf16[256,2048]{1,0:T(8,128)(2,1)S(1)} %pad_maximum_fusion.2), channel_id=1, source_target_pairs={{0,4},{1,3},{2,6},{3,1},{4,0},{5,7},{6,2},{7,5},{8,12},{9,11},{10,... | collective-permute-start | bytes 3145736 | tf_op jit(solution)/shard_map/ppermute | solution.py:46
  104.7 15.9 %collective-permute-start.9 = (bf16[512,512]{1,0:T(8,128)(2,1)S(1)}, bf16[512,512]{1,0:T(8,128)(2,1)S(1)}, u32[]{:S(2)}, u32[]{:S(2)}) collective-permute-start(bf16[512,512]{1,0:T(8,128)(2,1)S(1)} %slice.169), channel_id=1, source_target_pairs={{0,2},{1,9},{2,0},{3,11},{4,6},{5,13},{6,4},{7,15},{8,10},{9,1},{1... | collective-permute-start | bytes 1572872 | tf_op jit(solution)/shard_map/ppermute | solution.py:46
  107.8 20.6 %collective-permute-start.12 = (bf16[512,256]{1,0:T(8,128)(2,1)S(1)}, bf16[512,256]{1,0:T(8,128)(2,1)S(1)}, u32[]{:S(2)}, u32[]{:S(2)}) collective-permute-start(bf16[512,256]{1,0:T(8,128)(2,1)S(1)} %slice.170), channel_id=1, source_target_pairs={{0,4},{1,9},{2,6},{3,11},{4,0},{5,13},{6,2},{7,15},{8,12},{9,1},{1... | collective-permute-start | bytes 786440 | tf_op jit(solution)/shard_map/ppermute | solution.py:46
  121.5 2.2 %copy-start.2 = (bf16[4096,512]{1,0:T(8,128)(2,1)S(1)}, bf16[4096,512]{1,0:T(8,128)(2,1)}, u32[]{:S(2)}) copy-start(bf16[4096,512]{1,0:T(8,128)(2,1)} %inverse_ref.1) | copy-start | bytes 12582916
  121.5 12.9 %collective-permute-start.11 = (bf16[512,256]{1,0:T(8,128)(2,1)}, bf16[512,256]{1,0:T(8,128)(2,1)S(1)}, u32[]{:S(2)}, u32[]{:S(2)}) collective-permute-start(bf16[512,256]{1,0:T(8,128)(2,1)} %slice.171), channel_id=1, source_target_pairs={{0,8},{1,5},{2,10},{3,7},{4,12},{5,1},{6,14},{7,3},{8,0},{9,13},{1... | collective-permute-start | bytes 786440 | tf_op jit(solution)/shard_map/ppermute | solution.py:46
  123.7 4.7 %copy-start.3 = (s32[2,8]{1,0:T(2,128)S(1)}, s32[2,8]{1,0:T(2,128)}, u32[]{:S(2)}) copy-start(s32[2,8]{1,0:T(2,128)} %constant.47.clone) | copy-start | bytes 196
  125.5 8.9 %collective-permute-start.10 = (bf16[256,512]{1,0:T(8,128)(2,1)S(1)}, bf16[256,512]{1,0:T(8,128)(2,1)S(1)}, u32[]{:S(2)}, u32[]{:S(2)}) collective-permute-start(bf16[256,512]{1,0:T(8,128)(2,1)S(1)} %shard_map.88.own_ref), channel_id=1, source_target_pairs={{0,1},{1,0},{2,3},{3,2},{4,5},{5,4},{6,7},{7,6},{8,9},{9,8},{10,11... | collective-permute-start | bytes 786440 | tf_op jit(solution)/shard_map/ppermute | solution.py:248
  135.8 6.7 %collective-permute-start.13 = (bf16[64,512]{1,0:T(8,128)(2,1)S(1)}, bf16[64,512]{1,0:T(8,128)(2,1)S(1)}, u32[]{:S(2)}, u32[]{:S(2)}) collective-permute-start(bf16[64,512]{1,0:T(8,128)(2,1)S(1)} %get-tuple-element.76), channel_id=1, source_target_pairs={{0,8},{2,10},{4,12},{6,14},{8,0},{10,2},{12,4},{14,6},{1,9},{3,11}... | collective-permute-start | bytes 196616 | tf_op jit(solution)/shard_map/ppermute | solution.py:279
  135.8 8.2 %collective-permute-start.14 = (bf16[64,512]{1,0:T(8,128)(2,1)S(1)}, bf16[64,512]{1,0:T(8,128)(2,1)S(1)}, u32[]{:S(2)}, u32[]{:S(2)}) collective-permute-start(bf16[64,512]{1,0:T(8,128)(2,1)S(1)} %get-tuple-element.77), channel_id=1, source_target_pairs={{0,4},{2,6},{4,0},{6,2},{8,12},{10,14},{12,8},{14,10},{1,3},{3,1},... | collective-permute-start | bytes 196616 | tf_op jit(solution)/shard_map/ppermute | solution.py:279
  137.5 9.5 %collective-permute-start.15 = (bf16[64,512]{1,0:T(8,128)(2,1)S(1)}, bf16[64,512]{1,0:T(8,128)(2,1)S(1)}, u32[]{:S(2)}, u32[]{:S(2)}) collective-permute-start(bf16[64,512]{1,0:T(8,128)(2,1)S(1)} %get-tuple-element.78), channel_id=1, source_target_pairs={{0,12},{2,14},{4,8},{6,10},{8,4},{10,6},{12,0},{14,2},{1,11},{3,9}... | collective-permute-start | bytes 196616 | tf_op jit(solution)/shard_map/ppermute | solution.py:279
  140.2 6.8 %collective-permute-start.16 = (bf16[64,512]{1,0:T(8,128)(2,1)S(1)}, bf16[64,512]{1,0:T(8,128)(2,1)S(1)}, u32[]{:S(2)}, u32[]{:S(2)}) collective-permute-start(bf16[64,512]{1,0:T(8,128)(2,1)S(1)} %get-tuple-element.79), channel_id=1, source_target_pairs={{0,2},{2,0},{4,6},{6,4},{8,10},{10,8},{12,14},{14,12},{1,5},{3,7},... | collective-permute-start | bytes 196616 | tf_op jit(solution)/shard_map/ppermute | solution.py:279
  140.9 7.6 %collective-permute-start.17 = (bf16[64,512]{1,0:T(8,128)(2,1)S(1)}, bf16[64,512]{1,0:T(8,128)(2,1)S(1)}, u32[]{:S(2)}, u32[]{:S(2)}) collective-permute-start(bf16[64,512]{1,0:T(8,128)(2,1)S(1)} %get-tuple-element.80), channel_id=1, source_target_pairs={{0,10},{2,8},{4,14},{6,12},{8,2},{10,0},{12,6},{14,4},{1,13},{3,15... | collective-permute-start | bytes 196616 | tf_op jit(solution)/shard_map/ppermute | solution.py:279
  142.4 6.3 %collective-permute-start.18 = (bf16[64,512]{1,0:T(8,128)(2,1)S(1)}, bf16[64,512]{1,0:T(8,128)(2,1)S(1)}, u32[]{:S(2)}, u32[]{:S(2)}) collective-permute-start(bf16[64,512]{1,0:T(8,128)(2,1)S(1)} %get-tuple-element.81), channel_id=1, source_target_pairs={{0,6},{2,4},{4,2},{6,0},{8,14},{10,12},{12,10},{14,8},{1,7},{3,5},... | collective-permute-start | bytes 196616 | tf_op jit(solution)/shard_map/ppermute | solution.py:279
  144.0 7.0 %collective-permute-start.19 = (bf16[64,512]{1,0:T(8,128)(2,1)S(1)}, bf16[64,512]{1,0:T(8,128)(2,1)S(1)}, u32[]{:S(2)}, u32[]{:S(2)}) collective-permute-start(bf16[64,512]{1,0:T(8,128)(2,1)S(1)} %get-tuple-element.82), channel_id=1, source_target_pairs={{0,14},{2,12},{4,10},{6,8},{8,6},{10,4},{12,2},{14,0},{1,15},{3,13... | collective-permute-start | bytes 196616 | tf_op jit(solution)/shard_map/ppermute | solution.py:279

commit v5 on v3

--- a/solution.py
+++ b/solution.py
@@ -270,7 +270,7 @@
 
     parts = made["SC"]
     value = parts[0]
-    for i in range(1, n):
+    for i in reversed(range(1, n)):
         pairs = [
             (p * cores + e, p_to * cores + e)
             for e in range(cores)

time: 152 us -> 152 us (level)
  transfers between devices with their start and end apart: 20 -> 20, of which waited for: 8 -> 9; matrix products, arithmetic and copies ran while one was open for 2% -> 2% of each run, Pallas kernels for 44% -> 44%
where the time goes in v5:
time: 152 us
  Pallas kernels  82.4 us (54%)
  starting transfers between devices  30.8 us (20%)
  waiting for transfers between devices  29.8 us (20%)
  other arithmetic  4.73 us (3%)
  local copies, waits for them, and re-layouts  3.59 us (2%)
    pallas_call x6, Pallas kernels, product(): pl.pallas_call(functools.partial(product_kernel, with_top), grid_spec=plt...  79.2 us
    ppermute x12, waiting for transfers between devices, swap(): return lax.ppermute(value, BOTH, self.perms[hop])  23.7 us
    ppermute x12, starting transfers between devices, swap(): return lax.ppermute(value, BOTH, self.perms[hop])  17.9 us
    ppermute x7, starting transfers between devices, on_device(): value = value + lax.ppermute(parts[i], BOTH, pairs).astype(F32)  8.95 us
    ppermute x7, waiting for transfers between devices, on_device(): value = value + lax.ppermute(parts[i], BOTH, pairs).astype(F32)  6.07 us
    ppermute x1, starting transfers between devices, run(): moving['E'] = lax.ppermute(made['F'], 'ex', swap_cores)  3.94 us
  transfers between devices with their start and end apart: 20, of which 9 were waited for; matrix products, arithmetic and copies ran while one was open for 2% of the time, Pallas kernels for 44%

profile of v5, /device:TPU:0, one launch (start us, length us, event | category | flops | bytes accessed | tf_op | source)
XLA Modules:
  0.0 151.7 jit_solution(520294743651105096)
XLA Ops:
  0.0 0.7 broadcast_multiply_fusion
  0.8 2.2 %copy-done = bf16[256,8192]{1,0:T(8,128)(2,1)S(1)} copy-done((bf16[256,8192]{1,0:T(8,128)(2,1)S(1)}, bf16[256,8192]{1,0:T(8,128)(2,1)}, u32[]{:S(2)}) %copy-start) | copy-done | bytes 4194328
  3.0 14.7 %shard_map.82 = (f32[256,2048]{1,0:T(8,128)S(1)}, f32[8,2048]{1,0:T(8,128)S(1)}) custom-call(s32[4]{0:T(128)S(1)} %get-tuple-element.93.blocks_ref, bf16[256,8192]{1,0:T(8,128)(2,1)S(1)} %copy-done, bf16[8192,4096]{1,0:T(8,128)(2,1)} %p_ref.11), custom_call_target="tpu_custom_call" | custom-call | flops 1024 | bytes 1024 | tf_op jit(solution)/shard_map/pallas_call | solution.py:65
  17.8 0.2 multiply_convert_fusion
  18.0 0.3 pad_maximum_fusion.1
  18.3 3.1 %collective-permute-start = (f16[272,2048]{1,0:T(8,128)(2,1)S(1)}, f16[272,2048]{1,0:T(8,128)(2,1)S(1)}, u32[]{:S(2)}, u32[]{:S(2)}) collective-permute-start(f16[272,2048]{1,0:T(8,128)(2,1)S(1)} %pad_maximum_fusion.1), channel_id=1, source_target_pairs={{0,4},{1,3},{2,6},{3,1},{4,0},{5,7},{6,2},{7,5},{8,12},{9,11},{10,... | collective-permute-start | bytes 3342344 | tf_op jit(solution)/shard_map/ppermute | solution.py:46
  21.4 15.2 %shard_map.83 = (f32[256,2048]{1,0:T(8,128)S(1)}, f32[8,2048]{1,0:T(8,128)S(1)}) custom-call(s32[4]{0:T(128)S(1)} %get-tuple-element.44.blocks_ref, bf16[256,8192]{1,0:T(8,128)(2,1)S(1)} %copy-done.1, bf16[8192,4096]{1,0:T(8,128)(2,1)} %p_ref.11), custom_call_target="tpu_custom_call" | custom-call | flops 1024 | bytes 1024 | tf_op jit(solution)/shard_map/pallas_call | solution.py:65
  36.7 0.4 multiply_add_fusion
  37.1 0.1 slice.159
  37.2 0.1 multiply_convert_fusion.1
  37.3 0.1 pad_maximum_fusion.3
  37.5 1.8 %collective-permute-start.1 = (f16[272,1024]{1,0:T(8,128)(2,1)S(1)}, f16[272,1024]{1,0:T(8,128)(2,1)S(1)}, u32[]{:S(2)}, u32[]{:S(2)}) collective-permute-start(f16[272,1024]{1,0:T(8,128)(2,1)S(1)} %pad_maximum_fusion.3), channel_id=1, source_target_pairs={{0,2},{1,9},{2,0},{3,11},{4,6},{5,13},{6,4},{7,15},{8,10},{9,1},{1... | collective-permute-start | bytes 1671176 | tf_op jit(solution)/shard_map/ppermute | solution.py:46
  39.3 12.3 %shard_map.84 = bf16[512,1024]{1,0:T(8,128)(2,1)S(1)} custom-call(s32[4]{0:T(128)S(1)} %get-tuple-element.49.blocks_ref, bf16[512,8192]{1,0:T(8,128)(2,1)S(1)} %bitcast.24, bf16[8192,4096]{1,0:T(8,128)(2,1)} %p_ref.11), custom_call_target="tpu_custom_call" | custom-call | flops 1024 | bytes 1024 | tf_op jit(solution)/shard_map/pallas_call | solution.py:65
  51.6 0.2 slice_add_fusion.2
  52.0 0.4 collective-permute-start.4
  52.4 2.8 %collective-permute-start.2 = (f16[272,512]{1,0:T(8,128)(2,1)S(1)}, f16[272,512]{1,0:T(8,128)(2,1)S(1)}, u32[]{:S(2)}, u32[]{:S(2)}) collective-permute-start(f16[272,512]{1,0:T(8,128)(2,1)S(1)} %pad_maximum_fusion.5), channel_id=1, source_target_pairs={{0,8},{1,5},{2,10},{3,7},{4,12},{5,1},{6,14},{7,3},{8,0},{9,13},{1... | collective-permute-start | bytes 835592 | tf_op jit(solution)/shard_map/ppermute | solution.py:46
  55.2 12.3 %shard_map.85 = f32[512,1024]{1,0:T(8,128)S(1)} custom-call(s32[4]{0:T(128)S(1)} %get-tuple-element.53.blocks_ref, bf16[512,8192]{1,0:T(8,128)(2,1)S(1)} %bitcast.24, bf16[8192,4096]{1,0:T(8,128)(2,1)} %p_ref.11), custom_call_target="tpu_custom_call" | custom-call | flops 1024 | bytes 1024 | tf_op jit(solution)/shard_map/pallas_call | solution.py:65
  67.7 0.2 collective-permute-start.3
  67.9 0.4 convert_add_fusion.1
  68.4 2.8 %collective-permute-start.6 = (bf16[512,512]{1,0:T(8,128)(2,1)S(1)}, bf16[512,512]{1,0:T(8,128)(2,1)S(1)}, u32[]{:S(2)}, u32[]{:S(2)}) collective-permute-start(bf16[512,512]{1,0:T(8,128)(2,1)S(1)} %slice.166), channel_id=1, source_target_pairs={{0,8},{1,3},{2,10},{3,1},{4,12},{5,7},{6,14},{7,5},{8,0},{9,11},{1... | collective-permute-start | bytes 1572872 | tf_op jit(solution)/shard_map/ppermute | solution.py:46
  71.3 12.3 %shard_map.86 = bf16[512,1024]{1,0:T(8,128)(2,1)S(1)} custom-call(s32[4]{0:T(128)S(1)} %get-tuple-element.57.blocks_ref, bf16[512,8192]{1,0:T(8,128)(2,1)S(1)} %bitcast.24, bf16[8192,4096]{1,0:T(8,128)(2,1)} %p_ref.11), custom_call_target="tpu_custom_call" | custom-call | flops 1024 | bytes 1024 | tf_op jit(solution)/shard_map/pallas_call | solution.py:65
  83.6 1.7 %collective-permute-start.8 = (bf16[512,1024]{1,0:T(8,128)(2,1)S(1)}, bf16[512,1024]{1,0:T(8,128)(2,1)S(1)}, u32[]{:S(2)}, u32[]{:S(2)}) collective-permute-start(bf16[512,1024]{1,0:T(8,128)(2,1)S(1)} %shard_map.86), channel_id=1, source_target_pairs={{0,4},{1,3},{2,6},{3,1},{4,0},{5,7},{6,2},{7,5},{8,12},{9,11},{10,... | collective-permute-start | bytes 3145736 | tf_op jit(solution)/shard_map/ppermute | solution.py:46
  85.3 1.6 %collective-permute-start.5 = (bf16[256,1024]{1,0:T(8,128)(2,1)S(1)}, bf16[256,1024]{1,0:T(8,128)(2,1)S(1)}, u32[]{:S(2)}, u32[]{:S(2)}) collective-permute-start(bf16[256,1024]{1,0:T(8,128)(2,1)S(1)} %pad_maximum_fusion.4), channel_id=1, source_target_pairs={{0,2},{1,9},{2,0},{3,11},{4,6},{5,13},{6,4},{7,15},{8,10},{9,1},{1... | collective-permute-start | bytes 1572872 | tf_op jit(solution)/shard_map/ppermute | solution.py:46
  86.9 12.5 %shard_map.87 = f32[512,1024]{1,0:T(8,128)S(1)} custom-call(s32[4]{0:T(128)S(1)} %get-tuple-element.59.blocks_ref, bf16[512,8192]{1,0:T(8,128)(2,1)S(1)} %bitcast.24, bf16[8192,4096]{1,0:T(8,128)(2,1)} %p_ref.11), custom_call_target="tpu_custom_call" | custom-call | flops 1024 | bytes 1024 | tf_op jit(solution)/shard_map/pallas_call | solution.py:65
  99.4 0.2 slice_add_fusion.1
  99.7 0.5 collective-permute-start.7
  100.2 3.2 %collective-permute-done.8 = bf16[512,1024]{1,0:T(8,128)(2,1)S(1)} collective-permute-done((bf16[512,1024]{1,0:T(8,128)(2,1)S(1)}, bf16[512,1024]{1,0:T(8,128)(2,1)S(1)}, u32[]{:S(2)}, u32[]{:S(2)}) %collective-permute-start.8) | collective-permute-done | bytes 1048608 | tf_op jit(solution)/shard_map/ppermute | solution.py:46
  103.4 0.4 convert_add_fusion
  104.0 3.1 %collective-permute-start.9 = (bf16[512,512]{1,0:T(8,128)(2,1)S(1)}, bf16[512,512]{1,0:T(8,128)(2,1)S(1)}, u32[]{:S(2)}, u32[]{:S(2)}) collective-permute-start(bf16[512,512]{1,0:T(8,128)(2,1)S(1)} %slice.169), channel_id=1, source_target_pairs={{0,2},{1,9},{2,0},{3,11},{4,6},{5,13},{6,4},{7,15},{8,10},{9,1},{1... | collective-permute-start | bytes 1572872 | tf_op jit(solution)/shard_map/ppermute | solution.py:46
  107.2 11.9 %collective-permute-done.9 = bf16[512,512]{1,0:T(8,128)(2,1)S(1)} collective-permute-done((bf16[512,512]{1,0:T(8,128)(2,1)S(1)}, bf16[512,512]{1,0:T(8,128)(2,1)S(1)}, u32[]{:S(2)}, u32[]{:S(2)}) %collective-permute-start.9) | collective-permute-done | bytes 524320 | tf_op jit(solution)/shard_map/ppermute | solution.py:46
  119.0 0.2 slice_add_fusion
  119.2 0.7 slice.171
  119.9 2.3 %collective-permute-done.7 = bf16[256,2048]{1,0:T(8,128)(2,1)S(1)} collective-permute-done((bf16[256,2048]{1,0:T(8,128)(2,1)S(1)}, bf16[256,2048]{1,0:T(8,128)(2,1)S(1)}, u32[]{:S(2)}, u32[]{:S(2)}) %collective-permute-start.7) | collective-permute-done | bytes 1048608 | tf_op jit(solution)/shard_map/ppermute | solution.py:46
  122.2 0.2 pad_maximum_fusion.target_ref
  122.5 1.8 %shard_map.88.own_ref = bf16[256,512]{1,0:T(8,128)(2,1)S(1)} custom-call(s32[8]{0:T(128)S(1)} %bitcast.25, bf16[256,4096]{1,0:T(8,128)(2,1)S(1)} %pad_maximum_fusion.target_ref, bf16[4096,512]{1,0:T(8,128)(2,1)S(1)} %copy-done.2), custom_call_target="tpu_custom_call" | custom-call | flops 1024 | bytes 1024 | tf_op jit(solution)/shard_map/pallas_call | solution.py:101
  124.2 3.9 %collective-permute-start.10 = (bf16[256,512]{1,0:T(8,128)(2,1)S(1)}, bf16[256,512]{1,0:T(8,128)(2,1)S(1)}, u32[]{:S(2)}, u32[]{:S(2)}) collective-permute-start(bf16[256,512]{1,0:T(8,128)(2,1)S(1)} %shard_map.88.own_ref), channel_id=1, source_target_pairs={{0,1},{1,0},{2,3},{3,2},{4,5},{5,4},{6,7},{7,6},{8,9},{9,8},{10,11... | collective-permute-start | bytes 786440 | tf_op jit(solution)/shard_map/ppermute | solution.py:248
  128.3 6.3 %collective-permute-done.11.refs_1_ = bf16[512,256]{1,0:T(8,128)(2,1)S(1)} collective-permute-done((bf16[512,256]{1,0:T(8,128)(2,1)}, bf16[512,256]{1,0:T(8,128)(2,1)S(1)}, u32[]{:S(2)}, u32[]{:S(2)}) %collective-permute-start.11) | collective-permute-done | bytes 262176 | tf_op jit(solution)/shard_map/ppermute | solution.py:46
  134.6 1.3 shard_map.89
  136.0 1.7 %collective-permute-start.13 = (bf16[64,512]{1,0:T(8,128)(2,1)S(1)}, bf16[64,512]{1,0:T(8,128)(2,1)S(1)}, u32[]{:S(2)}, u32[]{:S(2)}) collective-permute-start(bf16[64,512]{1,0:T(8,128)(2,1)S(1)} %get-tuple-element.72), channel_id=1, source_target_pairs={{0,14},{2,12},{4,10},{6,8},{8,6},{10,4},{12,2},{14,0},{1,15},{3,13... | collective-permute-start | bytes 196616 | tf_op jit(solution)/shard_map/ppermute | solution.py:279
  137.7 3.7 %collective-permute-start.15 = (bf16[64,512]{1,0:T(8,128)(2,1)S(1)}, bf16[64,512]{1,0:T(8,128)(2,1)S(1)}, u32[]{:S(2)}, u32[]{:S(2)}) collective-permute-start(bf16[64,512]{1,0:T(8,128)(2,1)S(1)} %get-tuple-element.74), channel_id=1, source_target_pairs={{0,10},{2,8},{4,14},{6,12},{8,2},{10,0},{12,6},{14,4},{1,13},{3,15... | collective-permute-start | bytes 196616 | tf_op jit(solution)/shard_map/ppermute | solution.py:279
  141.4 1.4 collective-permute-start.16
  142.8 0.8 collective-permute-start.17
  143.7 2.2 %collective-permute-done.14 = bf16[64,512]{1,0:T(8,128)(2,1)S(1)} collective-permute-done((bf16[64,512]{1,0:T(8,128)(2,1)S(1)}, bf16[64,512]{1,0:T(8,128)(2,1)S(1)}, u32[]{:S(2)}, u32[]{:S(2)}) %collective-permute-start.14) | collective-permute-done | bytes 65568 | tf_op jit(solution)/shard_map/ppermute | solution.py:279
  145.9 1.3 collective-permute-start.19
  147.2 1.8 %collective-permute-done.17 = bf16[64,512]{1,0:T(8,128)(2,1)S(1)} collective-permute-done((bf16[64,512]{1,0:T(8,128)(2,1)S(1)}, bf16[64,512]{1,0:T(8,128)(2,1)S(1)}, u32[]{:S(2)}, u32[]{:S(2)}) %collective-permute-start.17) | collective-permute-done | bytes 65568 | tf_op jit(solution)/shard_map/ppermute | solution.py:279
  149.0 0.5 collective-permute-done.18
  149.5 1.5 collective-permute-done.19
  151.0 0.7 add_bitcast_fusion
  (56 shorter events, 1.3 us)
Async XLA Ops:
  0.8 2.2 %copy-start = (bf16[256,8192]{1,0:T(8,128)(2,1)S(1)}, bf16[256,8192]{1,0:T(8,128)(2,1)}, u32[]{:S(2)}) copy-start(bf16[256,8192]{1,0:T(8,128)(2,1)} %g_ref.7) | copy-start | bytes 12582916
  17.8 3.6 %copy-start.1 = (bf16[256,8192]{1,0:T(8,128)(2,1)S(1)}, bf16[256,8192]{1,0:T(8,128)(2,1)}, u32[]{:S(2)}) copy-start(bf16[256,8192]{1,0:T(8,128)(2,1)} %g_ref.7) | copy-start | bytes 12582916
  18.0 21.3 %slice-start = ((s8[8388608]{0:T(1024)(128)(4,1)}), s8[4194304]{0:T(1024)(128)(4,1)S(1)}, s32[]{:S(2)}) async-start(s8[8388608]{0:T(1024)(128)(4,1)} %bitcast.23), calls=%async_computation | async-start | bytes 8388608
  18.3 18.3 %collective-permute-start = (f16[272,2048]{1,0:T(8,128)(2,1)S(1)}, f16[272,2048]{1,0:T(8,128)(2,1)S(1)}, u32[]{:S(2)}, u32[]{:S(2)}) collective-permute-start(f16[272,2048]{1,0:T(8,128)(2,1)S(1)} %pad_maximum_fusion.1), channel_id=1, source_target_pairs={{0,4},{1,3},{2,6},{3,1},{4,0},{5,7},{6,2},{7,5},{8,12},{9,11},{10,... | collective-permute-start | bytes 3342344 | tf_op jit(solution)/shard_map/ppermute | solution.py:46
  21.4 17.9 %slice-start.1 = ((s8[8388608]{0:T(1024)(128)(4,1)}), s8[4194304]{0:T(1024)(128)(4,1)S(1)}, s32[]{:S(2)}) async-start(s8[8388608]{0:T(1024)(128)(4,1)} %bitcast.23), calls=%async_computation.1 | async-start | bytes 8388608
  37.5 14.1 %collective-permute-start.1 = (f16[272,1024]{1,0:T(8,128)(2,1)S(1)}, f16[272,1024]{1,0:T(8,128)(2,1)S(1)}, u32[]{:S(2)}, u32[]{:S(2)}) collective-permute-start(f16[272,1024]{1,0:T(8,128)(2,1)S(1)} %pad_maximum_fusion.3), channel_id=1, source_target_pairs={{0,2},{1,9},{2,0},{3,11},{4,6},{5,13},{6,4},{7,15},{8,10},{9,1},{1... | collective-permute-start | bytes 1671176 | tf_op jit(solution)/shard_map/ppermute | solution.py:46
  52.0 15.8 %collective-permute-start.4 = (bf16[512,1024]{1,0:T(8,128)(2,1)S(1)}, bf16[512,1024]{1,0:T(8,128)(2,1)S(1)}, u32[]{:S(2)}, u32[]{:S(2)}) collective-permute-start(bf16[512,1024]{1,0:T(8,128)(2,1)S(1)} %shard_map.84), channel_id=1, source_target_pairs={{0,2},{1,5},{2,0},{3,7},{4,6},{5,1},{6,4},{7,3},{8,10},{9,13},{10,... | collective-permute-start | bytes 3145736 | tf_op jit(solution)/shard_map/ppermute | solution.py:46
  52.4 15.1 %collective-permute-start.2 = (f16[272,512]{1,0:T(8,128)(2,1)S(1)}, f16[272,512]{1,0:T(8,128)(2,1)S(1)}, u32[]{:S(2)}, u32[]{:S(2)}) collective-permute-start(f16[272,512]{1,0:T(8,128)(2,1)S(1)} %pad_maximum_fusion.5), channel_id=1, source_target_pairs={{0,8},{1,5},{2,10},{3,7},{4,12},{5,1},{6,14},{7,3},{8,0},{9,13},{1... | collective-permute-start | bytes 835592 | tf_op jit(solution)/shard_map/ppermute | solution.py:46
  67.7 17.6 %collective-permute-start.3 = (bf16[256,512]{1,0:T(8,128)(2,1)S(1)}, bf16[256,512]{1,0:T(8,128)(2,1)S(1)}, u32[]{:S(2)}, u32[]{:S(2)}) collective-permute-start(bf16[256,512]{1,0:T(8,128)(2,1)S(1)} %fusion), channel_id=1, source_target_pairs={{0,8},{1,5},{2,10},{3,7},{4,12},{5,1},{6,14},{7,3},{8,0},{9,13},{1... | collective-permute-start | bytes 786440 | tf_op jit(solution)/shard_map/ppermute | solution.py:46
  68.4 31.0 %collective-permute-start.6 = (bf16[512,512]{1,0:T(8,128)(2,1)S(1)}, bf16[512,512]{1,0:T(8,128)(2,1)S(1)}, u32[]{:S(2)}, u32[]{:S(2)}) collective-permute-start(bf16[512,512]{1,0:T(8,128)(2,1)S(1)} %slice.166), channel_id=1, source_target_pairs={{0,8},{1,3},{2,10},{3,1},{4,12},{5,7},{6,14},{7,5},{8,0},{9,11},{1... | collective-permute-start | bytes 1572872 | tf_op jit(solution)/shard_map/ppermute | solution.py:46
  83.6 19.8 %collective-permute-start.8 = (bf16[512,1024]{1,0:T(8,128)(2,1)S(1)}, bf16[512,1024]{1,0:T(8,128)(2,1)S(1)}, u32[]{:S(2)}, u32[]{:S(2)}) collective-permute-start(bf16[512,1024]{1,0:T(8,128)(2,1)S(1)} %shard_map.86), channel_id=1, source_target_pairs={{0,4},{1,3},{2,6},{3,1},{4,0},{5,7},{6,2},{7,5},{8,12},{9,11},{10,... | collective-permute-start | bytes 3145736 | tf_op jit(solution)/shard_map/ppermute | solution.py:46
  85.3 14.3 %collective-permute-start.5 = (bf16[256,1024]{1,0:T(8,128)(2,1)S(1)}, bf16[256,1024]{1,0:T(8,128)(2,1)S(1)}, u32[]{:S(2)}, u32[]{:S(2)}) collective-permute-start(bf16[256,1024]{1,0:T(8,128)(2,1)S(1)} %pad_maximum_fusion.4), channel_id=1, source_target_pairs={{0,2},{1,9},{2,0},{3,11},{4,6},{5,13},{6,4},{7,15},{8,10},{9,1},{1... | collective-permute-start | bytes 1572872 | tf_op jit(solution)/shard_map/ppermute | solution.py:46
  99.7 22.5 %collective-permute-start.7 = (bf16[256,2048]{1,0:T(8,128)(2,1)S(1)}, bf16[256,2048]{1,0:T(8,128)(2,1)S(1)}, u32[]{:S(2)}, u32[]{:S(2)}) collective-permute-start(bf16[256,2048]{1,0:T(8,128)(2,1)S(1)} %pad_maximum_fusion.2), channel_id=1, source_target_pairs={{0,4},{1,3},{2,6},{3,1},{4,0},{5,7},{6,2},{7,5},{8,12},{9,11},{10,... | collective-permute-start | bytes 3145736 | tf_op jit(solution)/shard_map/ppermute | solution.py:46
  104.0 15.0 %collective-permute-start.9 = (bf16[512,512]{1,0:T(8,128)(2,1)S(1)}, bf16[512,512]{1,0:T(8,128)(2,1)S(1)}, u32[]{:S(2)}, u32[]{:S(2)}) collective-permute-start(bf16[512,512]{1,0:T(8,128)(2,1)S(1)} %slice.169), channel_id=1, source_target_pairs={{0,2},{1,9},{2,0},{3,11},{4,6},{5,13},{6,4},{7,15},{8,10},{9,1},{1... | collective-permute-start | bytes 1572872 | tf_op jit(solution)/shard_map/ppermute | solution.py:46
  107.1 21.2 %collective-permute-start.12 = (bf16[512,256]{1,0:T(8,128)(2,1)S(1)}, bf16[512,256]{1,0:T(8,128)(2,1)S(1)}, u32[]{:S(2)}, u32[]{:S(2)}) collective-permute-start(bf16[512,256]{1,0:T(8,128)(2,1)S(1)} %slice.170), channel_id=1, source_target_pairs={{0,4},{1,9},{2,6},{3,11},{4,0},{5,13},{6,2},{7,15},{8,12},{9,1},{1... | collective-permute-start | bytes 786440 | tf_op jit(solution)/shard_map/ppermute | solution.py:46
  119.9 2.5 %copy-start.2 = (bf16[4096,512]{1,0:T(8,128)(2,1)S(1)}, bf16[4096,512]{1,0:T(8,128)(2,1)}, u32[]{:S(2)}) copy-start(bf16[4096,512]{1,0:T(8,128)(2,1)} %inverse_ref.1) | copy-start | bytes 12582916
  119.9 14.7 %collective-permute-start.11 = (bf16[512,256]{1,0:T(8,128)(2,1)}, bf16[512,256]{1,0:T(8,128)(2,1)S(1)}, u32[]{:S(2)}, u32[]{:S(2)}) collective-permute-start(bf16[512,256]{1,0:T(8,128)(2,1)} %slice.171), channel_id=1, source_target_pairs={{0,8},{1,5},{2,10},{3,7},{4,12},{5,1},{6,14},{7,3},{8,0},{9,13},{1... | collective-permute-start | bytes 786440 | tf_op jit(solution)/shard_map/ppermute | solution.py:46
  122.4 5.7 %copy-start.3 = (s32[2,8]{1,0:T(2,128)S(1)}, s32[2,8]{1,0:T(2,128)}, u32[]{:S(2)}) copy-start(s32[2,8]{1,0:T(2,128)} %constant.47.clone) | copy-start | bytes 196
  124.2 10.4 %collective-permute-start.10 = (bf16[256,512]{1,0:T(8,128)(2,1)S(1)}, bf16[256,512]{1,0:T(8,128)(2,1)S(1)}, u32[]{:S(2)}, u32[]{:S(2)}) collective-permute-start(bf16[256,512]{1,0:T(8,128)(2,1)S(1)} %shard_map.88.own_ref), channel_id=1, source_target_pairs={{0,1},{1,0},{2,3},{3,2},{4,5},{5,4},{6,7},{7,6},{8,9},{9,8},{10,11... | collective-permute-start | bytes 786440 | tf_op jit(solution)/shard_map/ppermute | solution.py:248
  136.0 7.7 %collective-permute-start.13 = (bf16[64,512]{1,0:T(8,128)(2,1)S(1)}, bf16[64,512]{1,0:T(8,128)(2,1)S(1)}, u32[]{:S(2)}, u32[]{:S(2)}) collective-permute-start(bf16[64,512]{1,0:T(8,128)(2,1)S(1)} %get-tuple-element.72), channel_id=1, source_target_pairs={{0,14},{2,12},{4,10},{6,8},{8,6},{10,4},{12,2},{14,0},{1,15},{3,13... | collective-permute-start | bytes 196616 | tf_op jit(solution)/shard_map/ppermute | solution.py:279
  137.7 8.1 %collective-permute-start.14 = (bf16[64,512]{1,0:T(8,128)(2,1)S(1)}, bf16[64,512]{1,0:T(8,128)(2,1)S(1)}, u32[]{:S(2)}, u32[]{:S(2)}) collective-permute-start(bf16[64,512]{1,0:T(8,128)(2,1)S(1)} %get-tuple-element.73), channel_id=1, source_target_pairs={{0,6},{2,4},{4,2},{6,0},{8,14},{10,12},{12,10},{14,8},{1,7},{3,5},... | collective-permute-start | bytes 196616 | tf_op jit(solution)/shard_map/ppermute | solution.py:279
  137.7 9.5 %collective-permute-start.15 = (bf16[64,512]{1,0:T(8,128)(2,1)S(1)}, bf16[64,512]{1,0:T(8,128)(2,1)S(1)}, u32[]{:S(2)}, u32[]{:S(2)}) collective-permute-start(bf16[64,512]{1,0:T(8,128)(2,1)S(1)} %get-tuple-element.74), channel_id=1, source_target_pairs={{0,10},{2,8},{4,14},{6,12},{8,2},{10,0},{12,6},{14,4},{1,13},{3,15... | collective-permute-start | bytes 196616 | tf_op jit(solution)/shard_map/ppermute | solution.py:279
  141.4 5.8 %collective-permute-start.16 = (bf16[64,512]{1,0:T(8,128)(2,1)S(1)}, bf16[64,512]{1,0:T(8,128)(2,1)S(1)}, u32[]{:S(2)}, u32[]{:S(2)}) collective-permute-start(bf16[64,512]{1,0:T(8,128)(2,1)S(1)} %get-tuple-element.75), channel_id=1, source_target_pairs={{0,2},{2,0},{4,6},{6,4},{8,10},{10,8},{12,14},{14,12},{1,5},{3,7},... | collective-permute-start | bytes 196616 | tf_op jit(solution)/shard_map/ppermute | solution.py:279
  142.8 6.2 %collective-permute-start.17 = (bf16[64,512]{1,0:T(8,128)(2,1)S(1)}, bf16[64,512]{1,0:T(8,128)(2,1)S(1)}, u32[]{:S(2)}, u32[]{:S(2)}) collective-permute-start(bf16[64,512]{1,0:T(8,128)(2,1)S(1)} %get-tuple-element.76), channel_id=1, source_target_pairs={{0,12},{2,14},{4,8},{6,10},{8,4},{10,6},{12,0},{14,2},{1,11},{3,9}... | collective-permute-start | bytes 196616 | tf_op jit(solution)/shard_map/ppermute | solution.py:279
  143.7 5.9 %collective-permute-start.18 = (bf16[64,512]{1,0:T(8,128)(2,1)S(1)}, bf16[64,512]{1,0:T(8,128)(2,1)S(1)}, u32[]{:S(2)}, u32[]{:S(2)}) collective-permute-start(bf16[64,512]{1,0:T(8,128)(2,1)S(1)} %get-tuple-element.77), channel_id=1, source_target_pairs={{0,4},{2,6},{4,0},{6,2},{8,12},{10,14},{12,8},{14,10},{1,3},{3,1},... | collective-permute-start | bytes 196616 | tf_op jit(solution)/shard_map/ppermute | solution.py:279
  145.9 5.2 %collective-permute-start.19 = (bf16[64,512]{1,0:T(8,128)(2,1)S(1)}, bf16[64,512]{1,0:T(8,128)(2,1)S(1)}, u32[]{:S(2)}, u32[]{:S(2)}) collective-permute-start(bf16[64,512]{1,0:T(8,128)(2,1)S(1)} %get-tuple-element.78), channel_id=1, source_target_pairs={{0,8},{2,10},{4,12},{6,14},{8,0},{10,2},{12,4},{14,6},{1,9},{3,11}... | collective-permute-start | bytes 196616 | tf_op jit(solution)/shard_map/ppermute | solution.py:279
